TPU v7x, 128 devices: a whole 4x4x4 slice. The times are simulated.
128 devices in a mesh: section: 8 (over y, core), dp: 16 (over z, x).
Axes of the slice: x: 4, y: 4, z: 4, core: 2. Of those that a mesh axis runs over, the one named last changes fastest.
Arguments:
- section_inputs: bfloat16 [8, 8, 512, 16384], P('section', None, 'dp'), may hold values from -6 to 6
- top_grad: bfloat16 [8, 512, 16384], P(None, 'dp'), may hold values from -6 to 6
- weights: bfloat16 [8, 16384, 2, 128], P('section', 'dp'), may hold values from -6 to 6
- first_moment: float32 [8, 16384, 2, 128], P('section', 'dp'), may hold values from -12 to 12
- second_moment: float32 [8, 16384, 2, 128], P('section', 'dp'), may hold values from 1 to 20
- block_list: int32 [8, 16, 16], P('section', 'dp'), may hold values from 0 to 15
- block_owner: int32 [8, 16, 16, 1], P('section', 'dp'), may hold values from 0 to 15; in each aligned block of 16 rows (0 to 15, 16 to 31, ..., all dimensions but the last counted through in order) at most 2 rows name the same one
Outputs:
- new_weights: bfloat16 [8, 16384, 2, 128], P('section', 'dp')
- new_first: float32 [8, 16384, 2, 128], P('section', 'dp')
- new_second: float32 [8, 16384, 2, 128], P('section', 'dp')
- rollout_blocks: bfloat16 [8, 16, 16, 2, 128, 128], P('section', 'dp')
- rollout_ids: int32 [8, 16, 16, 2], P('section', 'dp')
Inputs may be any that keep to these rules, and one draw needn't show every extreme that they name: `block_list`: a tile may be listed twice. `block_owner`: among the 16 entries of one device no owner is named more than 2 times, a bound that some block reaches.
All inputs are finite; a program needn't handle non-finite values.
Results may differ from a plain program's by a relative error of at most 0.035.
Values may be sent and summed in bfloat16 or wider, within the bound.
A program may use at most 192 MiB of HBM per device.

v0:
```python
import jax
import jax.numpy as jnp
from jax import lax
from jax.sharding import PartitionSpec as P

BS = 128
CAP = 2


beta_one = 0.9
beta_two = 0.999
correct_one = 1.0 - 0.9**10
correct_two = 1.0 - 0.999**10
learn_rate = 0.01
decay_rate = 0.1
adam_eps = 1e-08


def from_behind(block, axis, distance):
    devices = range(lax.axis_size(axis))
    route = [(i - distance, i) for i in devices if i - distance in devices]
    return lax.ppermute(block, axis, route)


def contract_rows(left, right):
    return lax.dot_general(
        left, right, (((0,), (0,)), ((), ())), preferred_element_type=jnp.float32
    )


def shards(section_inputs, top_grad, weights, first_moment, second_moment, block_list, block_owner):
    sections = lax.axis_size("section")
    section_pos = lax.axis_index("section")
    micro_count = section_inputs.shape[1]
    tok_rows = section_inputs.shape[2]
    model_width = section_inputs.shape[3]
    adapter_rank = weights.shape[3]
    scale_a = model_width ** (-0.5)
    scale_b = adapter_rank ** (-0.5)
    gathered = lax.all_gather(weights, "dp", axis=1, tiled=True)
    adapt_a = gathered[0, :, 0, :]
    adapt_b = gathered[0, :, 1, :]
    group_size = 1
    group_count = micro_count // group_size
    row_count = group_size * tok_rows
    inputs = section_inputs[0]
    is_last = section_pos == sections - 1
    turn_count = group_count + sections - 1

    def compute(step_no, received, stores):
        slot_index = step_no - (sections - 1 - section_pos)
        is_valid = (slot_index >= 0) & (slot_index < group_count)
        clipped = jnp.clip(slot_index, 0, group_count - 1)
        h_rows = lax.dynamic_index_in_dim(inputs, clipped, 0, keepdims=False)
        top_rows = lax.dynamic_index_in_dim(top_grad, clipped, 0, keepdims=False)
        incoming = jnp.where(is_last, top_rows, received)
        adapter_out = (
            jnp.dot(h_rows, adapt_a, preferred_element_type=jnp.float32) * scale_a
        ).astype(jnp.bfloat16)
        delta_mid = (
            jnp.dot(incoming, adapt_b, preferred_element_type=jnp.float32) * scale_b
        ).astype(jnp.bfloat16)
        spread = lax.dot_general(
            delta_mid, adapt_a, (((1,), (1,)), ((), ())), preferred_element_type=jnp.float32
        )
        back_grad = (incoming.astype(jnp.float32) + spread * scale_a).astype(jnp.bfloat16)
        new_stores = tuple(
            (
                lax.dynamic_update_index_in_dim(
                    buffer,
                    jnp.where(
                        is_valid,
                        fresh,
                        lax.dynamic_index_in_dim(buffer, clipped, 0, keepdims=False),
                    ),
                    clipped,
                    0,
                )
                for buffer, fresh in zip(stores, (incoming, adapter_out, delta_mid))
            )
        )
        return (back_grad, new_stores)

    empty_stores = (
        jnp.zeros((group_count, row_count, model_width), jnp.bfloat16),
        jnp.zeros((group_count, row_count, adapter_rank), jnp.bfloat16),
        jnp.zeros((group_count, row_count, adapter_rank), jnp.bfloat16),
    )
    first_state = compute(0, jnp.zeros((row_count, model_width), jnp.bfloat16), empty_stores)

    def advance(carry, step_no):
        previous, stores = carry
        received = from_behind(previous, "section", -1)
        return (compute(step_no, received, stores), None)

    token_total = micro_count * tok_rows
    half_rows = token_total // 2
    h_all = section_inputs[0].reshape(token_total, model_width)
    shard_rows = weights.shape[1]

    def half_term(stores, which):
        first_row = which * half_rows
        g_all = stores[0].reshape(token_total, model_width)
        out_all = stores[1].reshape(token_total, adapter_rank)
        mid_all = stores[2].reshape(token_total, adapter_rank)
        h_part = lax.slice_in_dim(h_all, first_row, first_row + half_rows, axis=0)
        g_part = lax.slice_in_dim(g_all, first_row, first_row + half_rows, axis=0)
        out_part = lax.slice_in_dim(out_all, first_row, first_row + half_rows, axis=0)
        mid_part = lax.slice_in_dim(mid_all, first_row, first_row + half_rows, axis=0)
        grad_a = contract_rows(h_part, mid_part) * scale_a
        grad_b = contract_rows(g_part, out_part) * scale_b
        return jnp.stack([grad_a, grad_b], axis=1)

    final_state, unused = lax.scan(advance, first_state, jnp.arange(1, turn_count, dtype=jnp.int32))
    stores = final_state[1]
    lower = lax.optimization_barrier(half_term(stores, 0).astype(jnp.bfloat16))
    upper = lax.optimization_barrier(half_term(stores, 1).astype(jnp.bfloat16))
    gradient = lax.psum_scatter(
        (lower.astype(jnp.float32) + upper.astype(jnp.float32)).astype(jnp.bfloat16),
        "dp",
        scatter_dimension=0,
        tiled=True,
    ).astype(jnp.float32)
    new_first = beta_one * first_moment[0] + (1.0 - beta_one) * gradient
    new_second = beta_two * second_moment[0] + (1.0 - beta_two) * gradient * gradient
    master = weights[0].astype(jnp.float32)
    update = new_first / correct_one / (jnp.sqrt(new_second / correct_two) + adam_eps)
    new_shard = (master - learn_rate * (update + decay_rate * master)).astype(jnp.bfloat16)
    row_blocks = shard_rows // BS
    col_blocks = adapter_rank // BS
    tiles = (
        new_shard.reshape(row_blocks, BS, 2, col_blocks, BS)
        .transpose(0, 2, 3, 1, 4)
        .reshape(-1, BS, BS)
    )
    tile_count = tiles.shape[0]
    chosen = block_list[0, 0]
    owners = block_owner[0, 0, :, 0]
    list_len = chosen.shape[0]
    dp_size = lax.axis_size("dp")
    positions = jnp.arange(list_len, dtype=jnp.int32)
    same_owner = (owners[None, :] == owners[:, None]) & (positions[None, :] < positions[:, None])
    place = jnp.sum(same_owner.astype(jnp.int32), axis=1)
    selector = (owners[None, None, :] == jnp.arange(dp_size, dtype=jnp.int32)[:, None, None]) & (
        place[None, None, :] == jnp.arange(CAP, dtype=jnp.int32)[None, :, None]
    )
    picked = jnp.take(tiles, chosen, axis=0)
    send_tiles = jnp.dot(
        selector.reshape(dp_size * CAP, list_len).astype(jnp.bfloat16),
        picked.reshape(list_len, BS * BS),
        preferred_element_type=jnp.float32,
    )
    send_tiles = send_tiles.astype(jnp.bfloat16).reshape(dp_size, CAP, BS, BS)
    global_ids = lax.axis_index("dp") * tile_count + chosen + 1
    send_ids = jnp.sum(selector.astype(jnp.int32) * global_ids[None, None, :], axis=2) - 1
    recv_tiles, recv_ids = (
        lax.all_to_all(send_tiles, "dp", split_axis=0, concat_axis=0, tiled=True),
        lax.all_to_all(send_ids, "dp", split_axis=0, concat_axis=0, tiled=True),
    )
    return (
        new_shard[None],
        new_first[None],
        new_second[None],
        recv_tiles[None, None],
        recv_ids[None, None],
    )


def solution(mesh):
    placed = (
        P("section", None, "dp", None),
        P(None, "dp", None),
        P("section", "dp", None, None),
        P("section", "dp", None, None),
        P("section", "dp", None, None),
        P("section", "dp", None),
        P("section", "dp", None, None),
    )
    return jax.shard_map(
        shards,
        mesh=mesh,
        in_specs=placed,
        out_specs=(
            P("section", "dp", None, None),
            P("section", "dp", None, None),
            P("section", "dp", None, None),
            P("section", "dp", None, None, None, None),
            P("section", "dp", None, None),
        ),
        check_vma=False,
    )
```

profile of v0, /device:TPU:0, one launch (start us, length us, event | category | flops | bytes accessed | tf_op | source)
XLA Modules:
  0.0 556.5 jit_solution(6708218695702198722)
XLA Ops:
  9.2 5.2 broadcast_in_dim.62
  17.2 3.5 fusion.46
  20.7 63.4 %all-gather.2.cloned.1.call-done = bf16[1,16384,2,128]{3,1,2,0:T(8,128)(2,1)} async-done(((bf16[1,1024,2,128]{3,1,2,0:T(8,128)(2,1)}), bf16[1,16384,2,128]{3,1,2,0:T(8,128)(2,1)}) %all-gather.2.cloned.1.call-update) | async-done | bytes 8388624 | tf_op jit(solution)/shard_map/all_gather | solution.py:40
  84.1 6.8 %slice_bitcast_fusion = (bf16[16384,128]{1,0:T(8,128)(2,1)}, bf16[16384,128]{1,0:T(8,128)(2,1)}) fusion(bf16[1,16384,2,128]{3,1,2,0:T(8,128)(2,1)} %all-gather.2.cloned.1.call-done), kind=kLoop, calls=%fused_computation.42 | loop fusion | bytes 16777216 | tf_op jit(solution)/shard_map/squeeze | solution.py:41
  99.7 284.1 %while.18 = (s32[]{:T(128)}, bf16[32,16384]{1,0:T(8,128)(2,1)S(1)}, bf16[8,32,16384]{2,1,0:T(8,128)(2,1)}, bf16[8,32,128]{2,1,0:T(8,128)(2,1)S(1)}, bf16[8,32,12...) while((s32[]{:T(128)}, bf16[32,16384]{1,0:T(8,128)(2,1)S(1)}, ...), condition=%wide.region_1.2_spmd, body=%wide.region_0.1_spmd.sunk | while | flops 405823488 | bytes 61950284 | solution.py:114
  116.6 3.4 fusion.74
  120.0 4.8 collective-permute-done
  137.2 8.8 %collective-permute-done = bf16[32,16384]{1,0:T(8,128)(2,1)S(1)} collective-permute-done((bf16[32,16384]{1,0:T(8,128)(2,1)S(1)}, bf16[32,16384]{1,0:T(8,128)(2,1)S(1)}, u32[]{:S(2)}, u32[]{:S(2)}) %collective-permute-start) | collective-permute-done | bytes 1048608 | tf_op jit(solution)/shard_map/while/body/eval_jaxpr/ppermute | solution.py:22
  155.0 3.4 fusion.74
  158.5 8.8 %collective-permute-done = bf16[32,16384]{1,0:T(8,128)(2,1)S(1)} collective-permute-done((bf16[32,16384]{1,0:T(8,128)(2,1)S(1)}, bf16[32,16384]{1,0:T(8,128)(2,1)S(1)}, u32[]{:S(2)}, u32[]{:S(2)}) %collective-permute-start) | collective-permute-done | bytes 1048608 | tf_op jit(solution)/shard_map/while/body/eval_jaxpr/ppermute | solution.py:22
  179.6 8.8 %collective-permute-done = bf16[32,16384]{1,0:T(8,128)(2,1)S(1)} collective-permute-done((bf16[32,16384]{1,0:T(8,128)(2,1)S(1)}, bf16[32,16384]{1,0:T(8,128)(2,1)S(1)}, u32[]{:S(2)}, u32[]{:S(2)}) %collective-permute-start) | collective-permute-done | bytes 1048608 | tf_op jit(solution)/shard_map/while/body/eval_jaxpr/ppermute | solution.py:22
  200.8 8.8 %collective-permute-done = bf16[32,16384]{1,0:T(8,128)(2,1)S(1)} collective-permute-done((bf16[32,16384]{1,0:T(8,128)(2,1)S(1)}, bf16[32,16384]{1,0:T(8,128)(2,1)S(1)}, u32[]{:S(2)}, u32[]{:S(2)}) %collective-permute-start) | collective-permute-done | bytes 1048608 | tf_op jit(solution)/shard_map/while/body/eval_jaxpr/ppermute | solution.py:22
  222.0 8.8 %collective-permute-done = bf16[32,16384]{1,0:T(8,128)(2,1)S(1)} collective-permute-done((bf16[32,16384]{1,0:T(8,128)(2,1)S(1)}, bf16[32,16384]{1,0:T(8,128)(2,1)S(1)}, u32[]{:S(2)}, u32[]{:S(2)}) %collective-permute-start) | collective-permute-done | bytes 1048608 | tf_op jit(solution)/shard_map/while/body/eval_jaxpr/ppermute | solution.py:22
  243.2 8.7 %collective-permute-done = bf16[32,16384]{1,0:T(8,128)(2,1)S(1)} collective-permute-done((bf16[32,16384]{1,0:T(8,128)(2,1)S(1)}, bf16[32,16384]{1,0:T(8,128)(2,1)S(1)}, u32[]{:S(2)}, u32[]{:S(2)}) %collective-permute-start) | collective-permute-done | bytes 1048608 | tf_op jit(solution)/shard_map/while/body/eval_jaxpr/ppermute | solution.py:22
  264.3 8.8 %collective-permute-done = bf16[32,16384]{1,0:T(8,128)(2,1)S(1)} collective-permute-done((bf16[32,16384]{1,0:T(8,128)(2,1)S(1)}, bf16[32,16384]{1,0:T(8,128)(2,1)S(1)}, u32[]{:S(2)}, u32[]{:S(2)}) %collective-permute-start) | collective-permute-done | bytes 1048608 | tf_op jit(solution)/shard_map/while/body/eval_jaxpr/ppermute | solution.py:22
  285.4 8.8 %collective-permute-done = bf16[32,16384]{1,0:T(8,128)(2,1)S(1)} collective-permute-done((bf16[32,16384]{1,0:T(8,128)(2,1)S(1)}, bf16[32,16384]{1,0:T(8,128)(2,1)S(1)}, u32[]{:S(2)}, u32[]{:S(2)}) %collective-permute-start) | collective-permute-done | bytes 1048608 | tf_op jit(solution)/shard_map/while/body/eval_jaxpr/ppermute | solution.py:22
  306.5 8.8 %collective-permute-done = bf16[32,16384]{1,0:T(8,128)(2,1)S(1)} collective-permute-done((bf16[32,16384]{1,0:T(8,128)(2,1)S(1)}, bf16[32,16384]{1,0:T(8,128)(2,1)S(1)}, u32[]{:S(2)}, u32[]{:S(2)}) %collective-permute-start) | collective-permute-done | bytes 1048608 | tf_op jit(solution)/shard_map/while/body/eval_jaxpr/ppermute | solution.py:22
  324.3 3.4 fusion.74
  327.7 8.8 %collective-permute-done = bf16[32,16384]{1,0:T(8,128)(2,1)S(1)} collective-permute-done((bf16[32,16384]{1,0:T(8,128)(2,1)S(1)}, bf16[32,16384]{1,0:T(8,128)(2,1)S(1)}, u32[]{:S(2)}, u32[]{:S(2)}) %collective-permute-start) | collective-permute-done | bytes 1048608 | tf_op jit(solution)/shard_map/while/body/eval_jaxpr/ppermute | solution.py:22
  348.8 8.8 %collective-permute-done = bf16[32,16384]{1,0:T(8,128)(2,1)S(1)} collective-permute-done((bf16[32,16384]{1,0:T(8,128)(2,1)S(1)}, bf16[32,16384]{1,0:T(8,128)(2,1)S(1)}, u32[]{:S(2)}, u32[]{:S(2)}) %collective-permute-start) | collective-permute-done | bytes 1048608 | tf_op jit(solution)/shard_map/while/body/eval_jaxpr/ppermute | solution.py:22
  366.5 3.4 fusion.74
  369.9 8.8 %collective-permute-done = bf16[32,16384]{1,0:T(8,128)(2,1)S(1)} collective-permute-done((bf16[32,16384]{1,0:T(8,128)(2,1)S(1)}, bf16[32,16384]{1,0:T(8,128)(2,1)S(1)}, u32[]{:S(2)}, u32[]{:S(2)}) %collective-permute-start) | collective-permute-done | bytes 1048608 | tf_op jit(solution)/shard_map/while/body/eval_jaxpr/ppermute | solution.py:22
  383.9 5.6 %fusion.16 = bf16[16384,1,128]{0,2,1:T(8,128)(2,1)} fusion(bf16[8,32,16384]{2,1,0:T(8,128)(2,1)} %get-tuple-element.146, bf16[8,32,128]{2,1,0:T(8,128)(2,1)S(1)} %get-tuple-element.147), kind=kOutput, calls=%fused_computation.33 | convolution fusion | flops 541065216 | bytes 12615680 | tf_op jit(solution)/shard_map/dot_general | solution.py:26
  389.5 3.5 fusion.17
  396.2 7.5 %pad_maximum_fusion = bf16[16384,2,128]{0,2,1:T(8,128)(2,1)} fusion(bf16[16384,1,128]{0,2,1:T(8,128)(2,1)} %fusion.16, bf16[16384,1,128]{0,2,1:T(8,128)(2,1)} %fusion.15), kind=kLoop, calls=%fused_computation.40 | loop fusion | flops 4194304 | bytes 16777216 | tf_op jit(solution)/shard_map/stack | solution.py:112
  403.7 5.5 fusion.14
  409.2 6.2 %pad_maximum_fusion.1 = bf16[16384,2,128]{0,2,1:T(8,128)(2,1)} fusion(bf16[16384,1,128]{0,2,1:T(8,128)(2,1)S(1)} %fusion.17, bf16[16384,1,128]{0,2,1:T(8,128)(2,1)} %fusion.14), kind=kLoop, calls=%fused_computation.41 | loop fusion | flops 4194304 | bytes 16777216 | tf_op jit(solution)/shard_map/stack | solution.py:112
  415.4 9.5 %add_convert_fusion.1 = bf16[16384,2,128]{0,2,1:T(8,128)(2,1)} fusion(bf16[16384,2,128]{0,2,1:T(8,128)(2,1)} %pad_maximum_fusion.1, bf16[16384,2,128]{0,2,1:T(8,128)(2,1)} %pad_maximum_fusion), kind=kLoop, calls=%fused_computation.39 | loop fusion | flops 16777216 | bytes 25165824 | tf_op jit(solution)/shard_map/convert_element_type | solution.py:119
  426.8 5.3 all-to-all-start.1
  435.4 85.8 %reduce-scatter.2.cloned.1.call-done = bf16[1024,2,128]{0,2,1:T(8,128)(2,1)} async-done(((bf16[16384,2,128]{0,2,1:T(8,128)(2,1)}), bf16[1024,2,128]{0,2,1:T(8,128)(2,1)}) %reduce-scatter.2.cloned.1.call-update) | async-done | bytes 524304 | tf_op jit(solution)/shard_map/reduce_scatter | solution.py:118
  527.4 4.9 all-to-all-start
  537.6 11.1 %all-to-all-done = bf16[16,2,128,128]{3,2,1,0:T(8,128)(2,1)S(1)} async-done(((bf16[16,2,128,128]{3,2,1,0:T(8,128)(2,1)}), bf16[16,2,128,128]{3,2,1,0:T(8,128)(2,1)S(1)}, u32[]{:S(2)}, u32[]{:S(2)}) %all-to-all-start) | async-done | bytes 1048608 | tf_op jit(solution)/shard_map/all_to_all | solution.py:157
  (221 shorter events, 184.0 us)
Async XLA Ops:
  7.2 76.9 %all-gather.2.cloned.1.call-start = ((), (), s32[]{:S(2)}) async-start(), calls=%async_computation.3 | async-start | bytes 8912896 | tf_op jit(solution)/shard_map/all_gather | solution.py:40
  9.1 512.1 %reduce-scatter.2.cloned.1.call-start = ((), (), s32[]{:S(2)}) async-start(), calls=%async_computation.4 | async-start | bytes 8912896 | tf_op jit(solution)/shard_map/reduce_scatter | solution.py:118
  99.7 7.3 %collective-permute-start = (bf16[32,16384]{1,0:T(8,128)(2,1)S(1)}, bf16[32,16384]{1,0:T(8,128)(2,1)S(1)}, u32[]{:S(2)}, u32[]{:S(2)}) collective-permute-start(bf16[32,16384]{1,0:T(8,128)(2,1)S(1)} %get-tuple-element.313), channel_id=1, source_target_pairs={{16,0},{32,16},{48,32},{64,48},{80,64},{96,80},{112,96},{17,1},{33... | collective-permute-start | bytes 3145736 | tf_op jit(solution)/shard_map/while/body/eval_jaxpr/ppermute | solution.py:22
  112.7 12.2 %collective-permute-start = (bf16[32,16384]{1,0:T(8,128)(2,1)S(1)}, bf16[32,16384]{1,0:T(8,128)(2,1)S(1)}, u32[]{:S(2)}, u32[]{:S(2)}) collective-permute-start(bf16[32,16384]{1,0:T(8,128)(2,1)S(1)} %get-tuple-element.313), channel_id=1, source_target_pairs={{16,0},{32,16},{48,32},{64,48},{80,64},{96,80},{112,96},{17,1},{33... | collective-permute-start | bytes 3145736 | tf_op jit(solution)/shard_map/while/body/eval_jaxpr/ppermute | solution.py:22
  129.9 16.1 %collective-permute-start = (bf16[32,16384]{1,0:T(8,128)(2,1)S(1)}, bf16[32,16384]{1,0:T(8,128)(2,1)S(1)}, u32[]{:S(2)}, u32[]{:S(2)}) collective-permute-start(bf16[32,16384]{1,0:T(8,128)(2,1)S(1)} %get-tuple-element.313), channel_id=1, source_target_pairs={{16,0},{32,16},{48,32},{64,48},{80,64},{96,80},{112,96},{17,1},{33... | collective-permute-start | bytes 3145736 | tf_op jit(solution)/shard_map/while/body/eval_jaxpr/ppermute | solution.py:22
  133.8 15.8 %copy-start = (bf16[16384,128]{1,0:T(8,128)(2,1)S(1)}, bf16[16384,128]{1,0:T(8,128)(2,1)}, u32[]{:S(2)}) copy-start(bf16[16384,128]{1,0:T(8,128)(2,1)} %get-tuple-element.338) | copy-start | bytes 12582916 | tf_op jit(solution)/shard_map/while
  151.1 16.1 %collective-permute-start = (bf16[32,16384]{1,0:T(8,128)(2,1)S(1)}, bf16[32,16384]{1,0:T(8,128)(2,1)S(1)}, u32[]{:S(2)}, u32[]{:S(2)}) collective-permute-start(bf16[32,16384]{1,0:T(8,128)(2,1)S(1)} %get-tuple-element.313), channel_id=1, source_target_pairs={{16,0},{32,16},{48,32},{64,48},{80,64},{96,80},{112,96},{17,1},{33... | collective-permute-start | bytes 3145736 | tf_op jit(solution)/shard_map/while/body/eval_jaxpr/ppermute | solution.py:22
  155.0 15.0 %copy-start.1 = (bf16[16384,128]{1,0:T(8,128)(2,1)S(1)}, bf16[16384,128]{1,0:T(8,128)(2,1)}, u32[]{:S(2)}) copy-start(bf16[16384,128]{1,0:T(8,128)(2,1)} %get-tuple-element.337) | copy-start | bytes 12582916 | tf_op jit(solution)/shard_map/while
  155.0 15.8 %copy-start = (bf16[16384,128]{1,0:T(8,128)(2,1)S(1)}, bf16[16384,128]{1,0:T(8,128)(2,1)}, u32[]{:S(2)}) copy-start(bf16[16384,128]{1,0:T(8,128)(2,1)} %get-tuple-element.338) | copy-start | bytes 12582916 | tf_op jit(solution)/shard_map/while
  172.3 16.1 %collective-permute-start = (bf16[32,16384]{1,0:T(8,128)(2,1)S(1)}, bf16[32,16384]{1,0:T(8,128)(2,1)S(1)}, u32[]{:S(2)}, u32[]{:S(2)}) collective-permute-start(bf16[32,16384]{1,0:T(8,128)(2,1)S(1)} %get-tuple-element.313), channel_id=1, source_target_pairs={{16,0},{32,16},{48,32},{64,48},{80,64},{96,80},{112,96},{17,1},{33... | collective-permute-start | bytes 3145736 | tf_op jit(solution)/shard_map/while/body/eval_jaxpr/ppermute | solution.py:22
  176.2 15.8 %copy-start = (bf16[16384,128]{1,0:T(8,128)(2,1)S(1)}, bf16[16384,128]{1,0:T(8,128)(2,1)}, u32[]{:S(2)}) copy-start(bf16[16384,128]{1,0:T(8,128)(2,1)} %get-tuple-element.338) | copy-start | bytes 12582916 | tf_op jit(solution)/shard_map/while
  193.5 16.1 %collective-permute-start = (bf16[32,16384]{1,0:T(8,128)(2,1)S(1)}, bf16[32,16384]{1,0:T(8,128)(2,1)S(1)}, u32[]{:S(2)}, u32[]{:S(2)}) collective-permute-start(bf16[32,16384]{1,0:T(8,128)(2,1)S(1)} %get-tuple-element.313), channel_id=1, source_target_pairs={{16,0},{32,16},{48,32},{64,48},{80,64},{96,80},{112,96},{17,1},{33... | collective-permute-start | bytes 3145736 | tf_op jit(solution)/shard_map/while/body/eval_jaxpr/ppermute | solution.py:22
  197.4 15.8 %copy-start = (bf16[16384,128]{1,0:T(8,128)(2,1)S(1)}, bf16[16384,128]{1,0:T(8,128)(2,1)}, u32[]{:S(2)}) copy-start(bf16[16384,128]{1,0:T(8,128)(2,1)} %get-tuple-element.338) | copy-start | bytes 12582916 | tf_op jit(solution)/shard_map/while
  214.7 16.1 %collective-permute-start = (bf16[32,16384]{1,0:T(8,128)(2,1)S(1)}, bf16[32,16384]{1,0:T(8,128)(2,1)S(1)}, u32[]{:S(2)}, u32[]{:S(2)}) collective-permute-start(bf16[32,16384]{1,0:T(8,128)(2,1)S(1)} %get-tuple-element.313), channel_id=1, source_target_pairs={{16,0},{32,16},{48,32},{64,48},{80,64},{96,80},{112,96},{17,1},{33... | collective-permute-start | bytes 3145736 | tf_op jit(solution)/shard_map/while/body/eval_jaxpr/ppermute | solution.py:22
  218.6 15.0 %copy-start.1 = (bf16[16384,128]{1,0:T(8,128)(2,1)S(1)}, bf16[16384,128]{1,0:T(8,128)(2,1)}, u32[]{:S(2)}) copy-start(bf16[16384,128]{1,0:T(8,128)(2,1)} %get-tuple-element.337) | copy-start | bytes 12582916 | tf_op jit(solution)/shard_map/while
  218.6 15.8 %copy-start = (bf16[16384,128]{1,0:T(8,128)(2,1)S(1)}, bf16[16384,128]{1,0:T(8,128)(2,1)}, u32[]{:S(2)}) copy-start(bf16[16384,128]{1,0:T(8,128)(2,1)} %get-tuple-element.338) | copy-start | bytes 12582916 | tf_op jit(solution)/shard_map/while
  235.9 16.0 %collective-permute-start = (bf16[32,16384]{1,0:T(8,128)(2,1)S(1)}, bf16[32,16384]{1,0:T(8,128)(2,1)S(1)}, u32[]{:S(2)}, u32[]{:S(2)}) collective-permute-start(bf16[32,16384]{1,0:T(8,128)(2,1)S(1)} %get-tuple-element.313), channel_id=1, source_target_pairs={{16,0},{32,16},{48,32},{64,48},{80,64},{96,80},{112,96},{17,1},{33... | collective-permute-start | bytes 3145736 | tf_op jit(solution)/shard_map/while/body/eval_jaxpr/ppermute | solution.py:22
  239.8 15.6 %copy-start = (bf16[16384,128]{1,0:T(8,128)(2,1)S(1)}, bf16[16384,128]{1,0:T(8,128)(2,1)}, u32[]{:S(2)}) copy-start(bf16[16384,128]{1,0:T(8,128)(2,1)} %get-tuple-element.338) | copy-start | bytes 12582916 | tf_op jit(solution)/shard_map/while
  257.0 16.1 %collective-permute-start = (bf16[32,16384]{1,0:T(8,128)(2,1)S(1)}, bf16[32,16384]{1,0:T(8,128)(2,1)S(1)}, u32[]{:S(2)}, u32[]{:S(2)}) collective-permute-start(bf16[32,16384]{1,0:T(8,128)(2,1)S(1)} %get-tuple-element.313), channel_id=1, source_target_pairs={{16,0},{32,16},{48,32},{64,48},{80,64},{96,80},{112,96},{17,1},{33... | collective-permute-start | bytes 3145736 | tf_op jit(solution)/shard_map/while/body/eval_jaxpr/ppermute | solution.py:22
  260.8 15.7 %copy-start = (bf16[16384,128]{1,0:T(8,128)(2,1)S(1)}, bf16[16384,128]{1,0:T(8,128)(2,1)}, u32[]{:S(2)}) copy-start(bf16[16384,128]{1,0:T(8,128)(2,1)} %get-tuple-element.338) | copy-start | bytes 12582916 | tf_op jit(solution)/shard_map/while
  278.0 16.1 %collective-permute-start = (bf16[32,16384]{1,0:T(8,128)(2,1)S(1)}, bf16[32,16384]{1,0:T(8,128)(2,1)S(1)}, u32[]{:S(2)}, u32[]{:S(2)}) collective-permute-start(bf16[32,16384]{1,0:T(8,128)(2,1)S(1)} %get-tuple-element.313), channel_id=1, source_target_pairs={{16,0},{32,16},{48,32},{64,48},{80,64},{96,80},{112,96},{17,1},{33... | collective-permute-start | bytes 3145736 | tf_op jit(solution)/shard_map/while/body/eval_jaxpr/ppermute | solution.py:22
  281.9 15.7 %copy-start = (bf16[16384,128]{1,0:T(8,128)(2,1)S(1)}, bf16[16384,128]{1,0:T(8,128)(2,1)}, u32[]{:S(2)}) copy-start(bf16[16384,128]{1,0:T(8,128)(2,1)} %get-tuple-element.338) | copy-start | bytes 12582916 | tf_op jit(solution)/shard_map/while
  299.2 16.2 %collective-permute-start = (bf16[32,16384]{1,0:T(8,128)(2,1)S(1)}, bf16[32,16384]{1,0:T(8,128)(2,1)S(1)}, u32[]{:S(2)}, u32[]{:S(2)}) collective-permute-start(bf16[32,16384]{1,0:T(8,128)(2,1)S(1)} %get-tuple-element.313), channel_id=1, source_target_pairs={{16,0},{32,16},{48,32},{64,48},{80,64},{96,80},{112,96},{17,1},{33... | collective-permute-start | bytes 3145736 | tf_op jit(solution)/shard_map/while/body/eval_jaxpr/ppermute | solution.py:22
  303.1 15.8 %copy-start = (bf16[16384,128]{1,0:T(8,128)(2,1)S(1)}, bf16[16384,128]{1,0:T(8,128)(2,1)}, u32[]{:S(2)}) copy-start(bf16[16384,128]{1,0:T(8,128)(2,1)} %get-tuple-element.338) | copy-start | bytes 12582916 | tf_op jit(solution)/shard_map/while
  320.4 16.1 %collective-permute-start = (bf16[32,16384]{1,0:T(8,128)(2,1)S(1)}, bf16[32,16384]{1,0:T(8,128)(2,1)S(1)}, u32[]{:S(2)}, u32[]{:S(2)}) collective-permute-start(bf16[32,16384]{1,0:T(8,128)(2,1)S(1)} %get-tuple-element.313), channel_id=1, source_target_pairs={{16,0},{32,16},{48,32},{64,48},{80,64},{96,80},{112,96},{17,1},{33... | collective-permute-start | bytes 3145736 | tf_op jit(solution)/shard_map/while/body/eval_jaxpr/ppermute | solution.py:22
  324.3 15.6 %copy-start = (bf16[16384,128]{1,0:T(8,128)(2,1)S(1)}, bf16[16384,128]{1,0:T(8,128)(2,1)}, u32[]{:S(2)}) copy-start(bf16[16384,128]{1,0:T(8,128)(2,1)} %get-tuple-element.338) | copy-start | bytes 12582916 | tf_op jit(solution)/shard_map/while
  341.5 16.1 %collective-permute-start = (bf16[32,16384]{1,0:T(8,128)(2,1)S(1)}, bf16[32,16384]{1,0:T(8,128)(2,1)S(1)}, u32[]{:S(2)}, u32[]{:S(2)}) collective-permute-start(bf16[32,16384]{1,0:T(8,128)(2,1)S(1)} %get-tuple-element.313), channel_id=1, source_target_pairs={{16,0},{32,16},{48,32},{64,48},{80,64},{96,80},{112,96},{17,1},{33... | collective-permute-start | bytes 3145736 | tf_op jit(solution)/shard_map/while/body/eval_jaxpr/ppermute | solution.py:22
  345.3 15.7 %copy-start = (bf16[16384,128]{1,0:T(8,128)(2,1)S(1)}, bf16[16384,128]{1,0:T(8,128)(2,1)}, u32[]{:S(2)}) copy-start(bf16[16384,128]{1,0:T(8,128)(2,1)} %get-tuple-element.338) | copy-start | bytes 12582916 | tf_op jit(solution)/shard_map/while
  362.6 16.1 %collective-permute-start = (bf16[32,16384]{1,0:T(8,128)(2,1)S(1)}, bf16[32,16384]{1,0:T(8,128)(2,1)S(1)}, u32[]{:S(2)}, u32[]{:S(2)}) collective-permute-start(bf16[32,16384]{1,0:T(8,128)(2,1)S(1)} %get-tuple-element.313), channel_id=1, source_target_pairs={{16,0},{32,16},{48,32},{64,48},{80,64},{96,80},{112,96},{17,1},{33... | collective-permute-start | bytes 3145736 | tf_op jit(solution)/shard_map/while/body/eval_jaxpr/ppermute | solution.py:22
  366.5 15.6 %copy-start = (bf16[16384,128]{1,0:T(8,128)(2,1)S(1)}, bf16[16384,128]{1,0:T(8,128)(2,1)}, u32[]{:S(2)}) copy-start(bf16[16384,128]{1,0:T(8,128)(2,1)} %get-tuple-element.338) | copy-start | bytes 12582916 | tf_op jit(solution)/shard_map/while
  426.8 100.6 %all-to-all-start.1 = ((s32[16,1,2]{2,1,0:T(1,128)}), s32[16,1,2]{2,1,0:T(1,128)S(1)}, u32[]{:S(2)}, u32[]{:S(2)}) async-start(s32[16,1,2]{2,1,0:T(1,128)} %copy.52), calls=%async_computation.2 | async-start | bytes 16384 | tf_op jit(solution)/shard_map/all_to_all | solution.py:158
  527.4 21.3 %all-to-all-start = ((bf16[16,2,128,128]{3,2,1,0:T(8,128)(2,1)}), bf16[16,2,128,128]{3,2,1,0:T(8,128)(2,1)S(1)}, u32[]{:S(2)}, u32[]{:S(2)}) async-start(bf16[16,2,128,128]{3,2,1,0:T(8,128)(2,1)} %bitcast.58), calls=%async_computation.1 | async-start | bytes 2097152 | tf_op jit(solution)/shard_map/all_to_all | solution.py:157
  (21 other events, 228.6 us)
Sparse Core Ops, SparseCore 0:
  10.7 73.3 all-gather.1
  425.0 96.1 reduce-scatter.1
where the time goes:
time: 559 us; the launch traced here: 556 us
  waiting for transfers between devices  271 us (48%)
  matrix products  106 us (19%)
  other arithmetic  67.8 us (12%)
  local copies, waits for them, and re-layouts  59.3 us (11%)
  starting transfers between devices  28.3 us (5%)
  between operations  14.3 us (3%)
  loops' own time  10.6 us (2%)
    ppermute x14, waiting for transfers between devices, from_behind(): return lax.ppermute(block, axis, route)  110 us
    reduce_scatter x1, waiting for transfers between devices, shards(): lax.psum_scatter((lower.astype(jnp.float32) + upper.astype(jnp.float32))....  85.8 us
    all_gather x1, waiting for transfers between devices, shards(): gathered = lax.all_gather(weights, 'dp', axis=1, tiled=True)  63.4 us
    dot_general x15, matrix products, compute(): jnp.dot(h_rows, adapt_a, preferred_element_type=jnp.float32) * scale_a  49.9 us
    dynamic_update_slice x15, other arithmetic, compute(): lax.dynamic_update_index_in_dim(buffer, jnp.where(is_valid, fresh, lax.dy...  40.8 us
    dot_general x15, matrix products, compute(): lax.dot_general(delta_mid, adapt_a, (((1,), (1,)), ((), ())), preferred_e...  24.4 us
    dynamic_slice x28, local copies, waits for them, and re-layouts, compute(): lax.dynamic_index_in_dim(buffer, clipped, 0, keepdims=False)  18.3 us
    ppermute x14, starting transfers between devices, from_behind(): return lax.ppermute(block, axis, route)  18.1 us
  transfers between devices with their start and end apart: 18, of which 16 were waited for; matrix products, arithmetic and copies ran while one was open for 18% of the time, Pallas kernels for 0%

commit v1 on v0

v1 whole, which is shorter than its diff:
```python
import jax
import jax.numpy as jnp
from jax import lax
from jax.sharding import PartitionSpec as P

BS = 128
CAP = 2


beta_one = 0.9
beta_two = 0.999
correct_one = 1.0 - 0.9**10
correct_two = 1.0 - 0.999**10
learn_rate = 0.01
decay_rate = 0.1
adam_eps = 1e-08


def contract_rows(left, right):
    return lax.dot_general(
        left, right, (((0,), (0,)), ((), ())), preferred_element_type=jnp.float32
    )


def shards(section_inputs, top_grad, weights, first_moment, second_moment, block_list, block_owner):
    sections = lax.axis_size("section")
    section_pos = lax.axis_index("section")
    micro_count = section_inputs.shape[1]
    tok_rows = section_inputs.shape[2]
    model_width = section_inputs.shape[3]
    adapter_rank = weights.shape[3]
    scale_a = model_width ** (-0.5)
    scale_b = adapter_rank ** (-0.5)
    shard_rows = weights.shape[1]
    token_total = micro_count * tok_rows
    rows_a = weights[0, :, 0, :]
    rows_b = weights[0, :, 1, :]
    h_all = section_inputs[0].reshape(token_total, model_width)
    top_all = top_grad.reshape(token_total, model_width)
    every_a = lax.all_gather(rows_a, "section", axis=0)
    adapt_a = lax.all_gather(rows_a, "dp", axis=0, tiled=True)
    adapt_b = lax.all_gather(rows_b, "dp", axis=0, tiled=True)
    cross = lax.psum(
        lax.dot_general(every_a, rows_b, (((1,), (0,)), ((), ())), preferred_element_type=jnp.float32), "dp"
    )
    above = (jnp.arange(sections) > section_pos)[:, None, None]
    cross = jnp.where(above, cross * (scale_a * scale_b), 0.0).astype(jnp.bfloat16)
    adapter_out = (jnp.dot(h_all, adapt_a, preferred_element_type=jnp.float32) * scale_a).astype(jnp.bfloat16)
    direct = jnp.dot(top_all, adapt_b, preferred_element_type=jnp.float32) * scale_b
    every_direct = lax.all_gather(direct, "section", axis=0)
    every_cross = lax.all_gather(cross, "section", axis=0)
    deltas = [None] * sections
    for layer in range(sections - 1, -1, -1):
        total = every_direct[layer]
        for upper in range(layer + 1, sections):
            total = total + jnp.dot(deltas[upper], every_cross[layer, upper], preferred_element_type=jnp.float32)
        deltas[layer] = total.astype(jnp.bfloat16)
    deltas = jnp.stack(deltas)
    delta_mid = lax.dynamic_index_in_dim(deltas, section_pos, 0, keepdims=False)
    mixed = lax.psum(
        lax.dot_general(deltas, adapter_out, (((1,), (0,)), ((), ())), preferred_element_type=jnp.float32), "dp"
    )
    mixed = jnp.where(above, mixed, 0.0).astype(jnp.bfloat16)
    part_b = contract_rows(top_all, adapter_out).astype(jnp.bfloat16)
    part_a = contract_rows(h_all, delta_mid).astype(jnp.bfloat16)
    sum_b = lax.psum_scatter(part_b, "dp", scatter_dimension=0, tiled=True).astype(jnp.float32)
    sum_a = lax.psum_scatter(part_a, "dp", scatter_dimension=0, tiled=True).astype(jnp.float32)
    relayed = lax.dot_general(every_a, mixed, (((0, 2), (0, 1)), ((), ())), preferred_element_type=jnp.float32)
    gradient = jnp.stack([sum_a * scale_a, (sum_b + relayed * scale_a) * scale_b], axis=1)
    new_first = beta_one * first_moment[0] + (1.0 - beta_one) * gradient
    new_second = beta_two * second_moment[0] + (1.0 - beta_two) * gradient * gradient
    master = weights[0].astype(jnp.float32)
    update = new_first / correct_one / (jnp.sqrt(new_second / correct_two) + adam_eps)
    new_shard = (master - learn_rate * (update + decay_rate * master)).astype(jnp.bfloat16)
    row_blocks = shard_rows // BS
    col_blocks = adapter_rank // BS
    tiles = (
        new_shard.reshape(row_blocks, BS, 2, col_blocks, BS)
        .transpose(0, 2, 3, 1, 4)
        .reshape(-1, BS, BS)
    )
    tile_count = tiles.shape[0]
    chosen = block_list[0, 0]
    owners = block_owner[0, 0, :, 0]
    list_len = chosen.shape[0]
    dp_size = lax.axis_size("dp")
    positions = jnp.arange(list_len, dtype=jnp.int32)
    same_owner = (owners[None, :] == owners[:, None]) & (positions[None, :] < positions[:, None])
    place = jnp.sum(same_owner.astype(jnp.int32), axis=1)
    selector = (owners[None, None, :] == jnp.arange(dp_size, dtype=jnp.int32)[:, None, None]) & (
        place[None, None, :] == jnp.arange(CAP, dtype=jnp.int32)[None, :, None]
    )
    picked = jnp.take(tiles, chosen, axis=0)
    send_tiles = jnp.dot(
        selector.reshape(dp_size * CAP, list_len).astype(jnp.bfloat16),
        picked.reshape(list_len, BS * BS),
        preferred_element_type=jnp.float32,
    )
    send_tiles = send_tiles.astype(jnp.bfloat16).reshape(dp_size, CAP, BS, BS)
    global_ids = lax.axis_index("dp") * tile_count + chosen + 1
    send_ids = jnp.sum(selector.astype(jnp.int32) * global_ids[None, None, :], axis=2) - 1
    recv_tiles, recv_ids = (
        lax.all_to_all(send_tiles, "dp", split_axis=0, concat_axis=0, tiled=True),
        lax.all_to_all(send_ids, "dp", split_axis=0, concat_axis=0, tiled=True),
    )
    return (
        new_shard[None],
        new_first[None],
        new_second[None],
        recv_tiles[None, None],
        recv_ids[None, None],
    )


def solution(mesh):
    placed = (
        P("section", None, "dp", None),
        P(None, "dp", None),
        P("section", "dp", None, None),
        P("section", "dp", None, None),
        P("section", "dp", None, None),
        P("section", "dp", None),
        P("section", "dp", None, None),
    )
    return jax.shard_map(
        shards,
        mesh=mesh,
        in_specs=placed,
        out_specs=(
            P("section", "dp", None, None),
            P("section", "dp", None, None),
            P("section", "dp", None, None),
            P("section", "dp", None, None, None, None),
            P("section", "dp", None, None),
        ),
        check_vma=False,
    )
```

time: 559 us -> 496 us (0.89)
  blocking collectives: 0 us -> 82 us
  other arithmetic: 67.8 us -> 8.89 us
  matrix products: 106 us -> 61 us
  local copies, waits for them, and re-layouts: 59.3 us -> 26.2 us
  waiting for transfers between devices: 271 us -> 288 us
  starting transfers between devices: 28.3 us -> 12.4 us
  loops' own time: 10.6 us -> 0 us
    ppermute x14 -> x0, waiting for transfers between devices: 110 us -> none  [from_behind(): return lax.ppermute(block, axis, route)]
    all_gather x1 -> x5, waiting for transfers between devices: 63.4 us -> 165 us  [the longest x1 51.9 us: shards(): adapt_b = lax.all_gather(rows_b, 'dp', axis=0, tiled=True)]
    psum x0 -> x1, waiting for transfers between devices: none -> 85 us  [shards(): lax.psum(lax.dot_general(every_a, rows_b, (((1,), (0,)), ((), ())), prefe...]
    psum x0 -> x1, blocking collectives: none -> 82 us  [shards(): lax.psum(lax.dot_general(deltas, adapter_out, (((1,), (0,)), ((), ())), p...]
    reduce_scatter x1 -> x2, waiting for transfers between devices: 85.8 us -> 26 us  [the longest x1 26 us: shards(): lax.psum_scatter(part_a, 'dp', scatter_dimension=0, tiled=True)]
    dynamic_update_slice x15 -> x0, other arithmetic: 40.8 us -> none  [compute(): lax.dynamic_update_index_in_dim(buffer, jnp.where(is_valid, fresh, lax.dy...]
    dot_general x45 -> x33, matrix products: 87.2 us -> 47.2 us  [the longest x28 26.3 us: shards(): jnp.dot(deltas[upper], every_cross[layer, upper], preferred_element_type=...]
    dynamic_slice x42 -> x0, local copies, waits for them, and re-layouts: 26.6 us -> none  [the longest x28 18.3 us: compute(): lax.dynamic_index_in_dim(buffer, clipped, 0, keepdims=False)]
  transfers between devices with their start and end apart: 18 -> 10, of which waited for: 16 -> 8; matrix products, arithmetic and copies ran while one was open for 18% -> 18% of each run, Pallas kernels for 0% -> 0%
where the time goes in v1:
time: 496 us; the launch traced here: 494 us
  waiting for transfers between devices  288 us (58%)
  blocking collectives  82 us (17%)
  matrix products  61 us (12%)
  local copies, waits for them, and re-layouts  26.2 us (5%)
  between operations  14.6 us (3%)
  starting transfers between devices  12.4 us (2%)
  other arithmetic  8.89 us (2%)
    psum x1, waiting for transfers between devices, shards(): lax.psum(lax.dot_general(every_a, rows_b, (((1,), (0,)), ((), ())), prefe...  85 us
    psum x1, blocking collectives, shards(): lax.psum(lax.dot_general(deltas, adapter_out, (((1,), (0,)), ((), ())), p...  82 us
    all_gather x1, waiting for transfers between devices, shards(): adapt_b = lax.all_gather(rows_b, 'dp', axis=0, tiled=True)  51.9 us
    all_gather x1, waiting for transfers between devices, shards(): adapt_a = lax.all_gather(rows_a, 'dp', axis=0, tiled=True)  46.4 us
    all_gather x1, waiting for transfers between devices, shards(): every_a = lax.all_gather(rows_a, 'section', axis=0)  27.7 us
    dot_general x28, matrix products, shards(): jnp.dot(deltas[upper], every_cross[layer, upper], preferred_element_type=...  26.3 us
    reduce_scatter x1, waiting for transfers between devices, shards(): lax.psum_scatter(part_a, 'dp', scatter_dimension=0, tiled=True)  26 us
    all_gather x1, waiting for transfers between devices, shards(): every_direct = lax.all_gather(direct, 'section', axis=0)  25.9 us
  transfers between devices with their start and end apart: 10, of which 8 were waited for; matrix products, arithmetic and copies ran while one was open for 18% of the time, Pallas kernels for 0%

profile of v1, /device:TPU:0, one launch (start us, length us, event | category | flops | bytes accessed | tf_op | source)
XLA Modules:
  0.0 493.6 jit_solution(9918036632364873174)
XLA Ops:
  7.2 2.1 fusion.66
  10.2 27.7 %all-gather.15.cloned.1.call-done = bf16[8,1024,1,128]{3,1,2,0:T(8,128)(2,1)} async-done(((bf16[1,1024,1,128]{3,1,2,0:T(8,128)(2,1)}), bf16[8,1024,1,128]{3,1,2,0:T(8,128)(2,1)}) %all-gather.15.cloned.1.call-update) | async-done | bytes 2097168 | tf_op jit(solution)/shard_map/all_gather | solution.py:40
  38.0 3.1 fusion.8
  42.5 85.0 %all-reduce.3.cloned.1.call-done = f32[8,128,128]{2,1,0:T(8,128)} async-done(((f32[8,128,128]{2,1,0:T(8,128)}), f32[8,128,128]{2,1,0:T(8,128)}) %all-reduce.3.cloned.1.call-update) | async-done | bytes 524304 | tf_op jit(solution)/shard_map/psum | solution.py:43
  127.5 1.9 select_convert_fusion.1
  129.4 51.9 %all-gather.11.cloned.1.call-done = bf16[1,16384,1,128]{3,1,2,0:T(8,128)(2,1)} async-done(((bf16[1,1024,1,128]{3,1,2,0:T(8,128)(2,1)}), bf16[1,16384,1,128]{3,1,2,0:T(8,128)(2,1)}) %all-gather.11.cloned.1.call-update) | async-done | bytes 4194320 | tf_op jit(solution)/shard_map/all_gather | solution.py:42
  181.4 7.6 %fusion.26 = f32[256,128]{1,0:T(8,128)} fusion(bf16[256,16384]{1,0:T(8,128)(2,1)} %bitcast.242, bf16[1,16384,1,128]{3,1,2,0:T(8,128)(2,1)} %all-gather.11.cloned.1.call-done), kind=kOutput, calls=%fused_computation.22 | convolution fusion | flops 1073774592 | bytes 12713984 | tf_op jit(solution)/shard_map/dot_general | solution.py:49
  189.0 46.4 %all-gather.19.cloned.1.call-done = bf16[1,16384,1,128]{3,1,2,0:T(8,128)(2,1)} async-done(((bf16[1,1024,1,128]{3,1,2,0:T(8,128)(2,1)}), bf16[1,16384,1,128]{3,1,2,0:T(8,128)(2,1)}) %all-gather.19.cloned.1.call-update) | async-done | bytes 4194320 | tf_op jit(solution)/shard_map/all_gather | solution.py:41
  235.4 6.9 %fusion.32 = bf16[256,128]{1,0:T(8,128)(2,1)S(1)} fusion(bf16[256,16384]{1,0:T(8,128)(2,1)} %bitcast.244, bf16[1,16384,1,128]{3,1,2,0:T(8,128)(2,1)} %all-gather.19.cloned.1.call-done), kind=kOutput, calls=%fused_computation.52 | convolution fusion | flops 1073807360 | bytes 12648448 | tf_op jit(solution)/shard_map/dot_general | solution.py:48
  242.3 6.6 %fusion.1 = bf16[16384,128]{0,1:T(8,128)(2,1)} fusion(bf16[256,128]{1,0:T(8,128)(2,1)S(1)} %fusion.32, bf16[256,16384]{1,0:T(8,128)(2,1)} %bitcast.243), kind=kOutput, calls=%fused_computation.4 | convolution fusion | flops 1075838976 | bytes 12648448 | tf_op jit(solution)/shard_map/dot_general | solution.py:20
  249.0 13.4 %all-gather.17.cloned.1.call-done = bf16[64,128,128]{2,1,0:T(8,128)(2,1)} async-done(((bf16[8,128,128]{2,1,0:T(8,128)(2,1)}), bf16[64,128,128]{2,1,0:T(8,128)(2,1)}) %all-gather.17.cloned.1.call-update) | async-done | bytes 2097168 | tf_op jit(solution)/shard_map/all_gather | solution.py:51
  262.5 25.9 %all-gather.13.cloned.1.call-done = f32[2048,128]{1,0:T(8,128)} async-done(((f32[256,128]{1,0:T(8,128)}), f32[2048,128]{1,0:T(8,128)}) %all-gather.13.cloned.1.call-update) | async-done | bytes 1048592 | tf_op jit(solution)/shard_map/all_gather | solution.py:50
  315.8 6.7 %fusion = bf16[16384,128]{0,1:T(8,128)(2,1)} fusion(bf16[256,16384]{1,0:T(8,128)(2,1)} %bitcast.245, bf16[8,256,128]{2,1,0:T(8,128)(2,1)S(1)} %bitcast_dynamic-update-slice_fusion, s32[]{:T(128)S(6)} %select_n.42), kind=kOutput, calls=%fused_computation.3 | convolution fusion | flops 1075838976 | bytes 12648452 | tf_op jit(solution)/shard_map/dot_general | solution.py:20
  324.5 7.0 %all-to-all-start.1 = ((s32[16,1,2]{2,1,0:T(1,128)}), s32[16,1,2]{2,1,0:T(1,128)S(1)}, u32[]{:S(2)}, u32[]{:S(2)}) async-start(s32[16,1,2]{2,1,0:T(1,128)} %copy.79), calls=%async_computation.3 | async-start | bytes 16384 | tf_op jit(solution)/shard_map/all_to_all | solution.py:104
  332.0 1.3 copy.64
  333.3 2.3 copy.71
  336.8 2.7 copy.77
  339.6 1.4 fusion.57
  341.0 82.0 %all-reduce.4 = bf16[8,128,128]{2,1,0:T(8,128)(2,1)S(1)} all-reduce(f32[8,128,128]{2,1,0:T(8,128)S(1)} %fusion.57), channel_id=1, replica_groups=mesh['section'=8,'dp'=16] {'dp'}, use_global_device_ids=true, to_apply=%region_3.4 | all-reduce | flops 131072 | bytes 786432 | tf_op jit(solution)/shard_map/psum | solution.py:60
  423.0 1.9 fusion.23
  426.0 26.0 %reduce-scatter.3.cloned.1.call-done = bf16[1024,128]{0,1:T(8,128)(2,1)} async-done(((bf16[16384,128]{0,1:T(8,128)(2,1)}), bf16[1024,128]{0,1:T(8,128)(2,1)}) %reduce-scatter.3.cloned.1.call-update) | async-done | bytes 262160 | tf_op jit(solution)/shard_map/reduce_scatter | solution.py:67
  452.0 1.9 convert_multiply_fusion
  453.8 2.2 subtract_convert_fusion.1
  457.5 1.4 copy.74
  458.9 1.2 copy.89
  460.1 2.1 subtract_convert_fusion
  463.5 1.2 copy.97
  464.8 5.0 %all-to-all-start = ((bf16[16,2,128,128]{3,2,1,0:T(8,128)(2,1)}), bf16[16,2,128,128]{3,2,1,0:T(8,128)(2,1)S(1)}, u32[]{:S(2)}, u32[]{:S(2)}) async-start(bf16[16,2,128,128]{3,2,1,0:T(8,128)(2,1)} %bitcast.93), calls=%async_computation.2 | async-start | bytes 2097152 | tf_op jit(solution)/shard_map/all_to_all | solution.py:103
  470.4 2.0 copy.81
  472.4 1.3 copy.82
  473.7 1.3 copy.83
  475.0 10.7 %all-to-all-done = bf16[16,2,128,128]{3,2,1,0:T(8,128)(2,1)S(1)} async-done(((bf16[16,2,128,128]{3,2,1,0:T(8,128)(2,1)}), bf16[16,2,128,128]{3,2,1,0:T(8,128)(2,1)S(1)}, u32[]{:S(2)}, u32[]{:S(2)}) %all-to-all-start) | async-done | bytes 1048608 | tf_op jit(solution)/shard_map/all_to_all | solution.py:103
  (108 shorter events, 38.6 us)
Async XLA Ops:
  7.2 30.8 %all-gather.15.cloned.1.call-start = ((), (), s32[]{:S(2)}) async-start(), calls=%async_computation.9 | async-start | bytes 2359296 | tf_op jit(solution)/shard_map/all_gather | solution.py:40
  10.1 117.4 %all-reduce.3.cloned.1.call-start = ((), (), s32[]{:S(2)}) async-start(), calls=%async_computation.4 | async-start | bytes 1048576 | tf_op jit(solution)/shard_map/psum | solution.py:43
  10.2 31.0 %copy-start.9 = (bf16[1,1024,1,128]{3,1,2,0:T(8,128)(2,1)}, bf16[1,1024,1,128]{3,1,2,0:T(8,128)(2,1)S(1)}, u32[]{:S(2)}) copy-start(bf16[1,1024,1,128]{3,1,2,0:T(8,128)(2,1)S(1)} %copy.91) | copy-start | bytes 786436
  41.1 140.2 %all-gather.11.cloned.1.call-start = ((), (), s32[]{:S(2)}) async-start(), calls=%async_computation.7 | async-start | bytes 4456448 | tf_op jit(solution)/shard_map/all_gather | solution.py:42
  41.9 193.6 %all-gather.19.cloned.1.call-start = ((), (), s32[]{:S(2)}) async-start(), calls=%async_computation.11 | async-start | bytes 4456448 | tf_op jit(solution)/shard_map/all_gather | solution.py:41
  42.4 220.0 %all-gather.17.cloned.1.call-start = ((), (), s32[]{:S(2)}) async-start(), calls=%async_computation.10 | async-start | bytes 2359296 | tf_op jit(solution)/shard_map/all_gather | solution.py:51
  129.4 159.0 %all-gather.13.cloned.1.call-start = ((), (), s32[]{:S(2)}) async-start(), calls=%async_computation.8 | async-start | bytes 1179648 | tf_op jit(solution)/shard_map/all_gather | solution.py:50
  188.9 234.1 %reduce-scatter.5.cloned.1.call-start = ((), (), s32[]{:S(2)}) async-start(), calls=%async_computation.6 | async-start | bytes 4456448 | tf_op jit(solution)/shard_map/reduce_scatter | solution.py:66
  249.0 203.0 %reduce-scatter.3.cloned.1.call-start = ((), (), s32[]{:S(2)}) async-start(), calls=%async_computation.5 | async-start | bytes 4456448 | tf_op jit(solution)/shard_map/reduce_scatter | solution.py:67
  288.4 6.4 %copy-start.8 = (f32[2048,128]{1,0:T(8,128)S(1)}, f32[2048,128]{1,0:T(8,128)}, u32[]{:S(2)}) copy-start(f32[2048,128]{1,0:T(8,128)} %all-gather.13.cloned.1.call-done) | copy-start | bytes 3145732
  315.0 0.8 copy-start.11
  322.5 0.7 copy-start.12
  322.5 0.8 copy-start.13
  322.5 9.0 %copy-start.1 = (bf16[1,1024,2,128]{3,2,1,0:T(2,128)(2,1)S(1)}, bf16[1,1024,2,128]{3,2,1,0:T(2,128)(2,1)}, u32[]{:S(2)}) copy-start(bf16[1,1024,2,128]{3,2,1,0:T(2,128)(2,1)} %param.9) | copy-start | bytes 1572868
  322.5 9.5 %copy-start.10 = (f32[1,1024,2,128]{3,2,1,0:T(2,128)S(1)}, f32[1,1024,2,128]{3,2,1,0:T(2,128)}, u32[]{:S(2)}) copy-start(f32[1,1024,2,128]{3,2,1,0:T(2,128)} %param.10) | copy-start | bytes 3145732
  324.5 140.2 %all-to-all-start.1 = ((s32[16,1,2]{2,1,0:T(1,128)}), s32[16,1,2]{2,1,0:T(1,128)S(1)}, u32[]{:S(2)}, u32[]{:S(2)}) async-start(s32[16,1,2]{2,1,0:T(1,128)} %copy.79), calls=%async_computation.3 | async-start | bytes 16384 | tf_op jit(solution)/shard_map/all_to_all | solution.py:104
  336.8 86.2 %copy-start = (bf16[8,1024,1,128]{3,1,2,0:T(8,128)(2,1)S(1)}, bf16[8,1024,1,128]{3,1,2,0:T(8,128)(2,1)}, u32[]{:S(2)}) copy-start(bf16[8,1024,1,128]{3,1,2,0:T(8,128)(2,1)} %all-gather.15.cloned.1.call-done) | copy-start | bytes 6291460
  425.0 28.9 %copy-start.5 = (f32[1,1024,2,128]{1,3,2,0:T(8,128)S(1)}, f32[1,1024,2,128]{1,3,2,0:T(8,128)}, u32[]{:S(2)}) copy-start(f32[1,1024,2,128]{1,3,2,0:T(8,128)} %copy.64) | copy-start | bytes 3145732
  425.0 28.9 %copy-start.6 = (f32[1,1024,2,128]{1,3,2,0:T(8,128)S(1)}, f32[1,1024,2,128]{1,3,2,0:T(8,128)}, u32[]{:S(2)}) copy-start(f32[1,1024,2,128]{1,3,2,0:T(8,128)} %copy.71) | copy-start | bytes 3145732
  456.1 1.2 copy-start.7
  457.5 2.6 copy-start.2
  464.7 7.7 %copy-start.4 = (f32[1,1024,2,128]{1,3,2,0:T(8,128)S(1)}, f32[1,1024,2,128]{1,3,2,0:T(8,128)}, u32[]{:S(2)}) copy-start(f32[1,1024,2,128]{1,3,2,0:T(8,128)} %get-tuple-element.28) | copy-start | bytes 3145732
  464.8 21.0 %all-to-all-start = ((bf16[16,2,128,128]{3,2,1,0:T(8,128)(2,1)}), bf16[16,2,128,128]{3,2,1,0:T(8,128)(2,1)S(1)}, u32[]{:S(2)}, u32[]{:S(2)}) async-start(bf16[16,2,128,128]{3,2,1,0:T(8,128)(2,1)} %bitcast.93), calls=%async_computation.2 | async-start | bytes 2097152 | tf_op jit(solution)/shard_map/all_to_all | solution.py:103
  469.8 3.9 copy-start.3
Sparse Core Ops, SparseCore 0:
  10.3 27.6 all-gather.14
  41.7 85.6 all-reduce.2
  130.4 50.8 all-gather.10
  184.1 51.2 all-gather.18
  237.7 24.7 all-gather.16
  264.7 23.6 all-gather.12
  292.1 78.4 reduce-scatter.4
  373.9 78.0 reduce-scatter.2

commit v2 on v1

v2 whole, which is shorter than its diff:
```python
import functools

import jax
import jax.numpy as jnp
from jax import lax
from jax.experimental import pallas as pl
from jax.experimental.pallas import tpu as pltpu
from jax.sharding import PartitionSpec as P

BS = 128
CAP = 2
RING = 4
GROUP = RING * RING

beta_one = 0.9
beta_two = 0.999
correct_one = 1.0 - 0.9**10
correct_two = 1.0 - 0.999**10
learn_rate = 0.01
decay_rate = 0.1
adam_eps = 1e-08

MESH = pl.DeviceIdType.MESH
F32 = jnp.float32
BF16 = jnp.bfloat16
DIRS = (1, -1)
SHIFTS = (0, 1, 3, 2)


def wrap(value):
    return lax.rem(value + 2 * RING, RING)


class Plane:
    def __init__(self):
        me = lax.axis_index("dp")
        self.me = me
        z, x = me // RING, lax.rem(me, RING)
        self.place = ((x, z), (z, x))

    def slot(self, half, first, second):
        i, j = self.place[half]
        i, j = wrap(i + first), wrap(j + second)
        return j * RING + i if half == 0 else i * RING + j

    def away(self, dz, dx):
        return self.slot(1, dz, dx)


class Gather:
    def __init__(self, plane, buf, send_sem, recv_sem):
        self.plane, self.buf, self.send_sem, self.recv_sem = plane, buf, send_sem, recv_sem
        self.rows = buf.shape[1]

    def part(self, half, piece):
        if piece is None:
            return pl.ds(half * (self.rows // 2), self.rows // 2)
        return pl.ds(half * (self.rows // 2) + piece * (self.rows // 4), self.rows // 4)

    def copy(self, half, kind, d, a, arriving):
        plane = self.plane
        dd = 0 if d == 1 else 1
        hop = -d if arriving else 0
        if kind == "F1":
            k, q, piece = dd, plane.slot(half, hop, 0), None
        elif kind == "F2":
            k, q, piece = 2 + dd, plane.slot(half, hop - d, 0), dd
        elif kind == "G1":
            k, q, piece = 4 + 2 * a + dd, plane.slot(half, a, hop), None
        else:
            k, q, piece = 12 + 2 * a + dd, plane.slot(half, a, hop - d), dd
        to = plane.slot(half, d, 0) if kind[0] == "F" else plane.slot(half, 0, d)
        where = self.buf.at[q, self.part(half, piece)]
        return pltpu.make_async_remote_copy(
            src_ref=where, dst_ref=where, send_sem=self.send_sem.at[0], recv_sem=self.recv_sem.at[half * 20 + k],
            device_id={"dp": to}, device_id_type=MESH,
        )

    def send(self, kind, a=0):
        for half in (0, 1):
            for d in DIRS:
                self.copy(half, kind, d, a, False).start()

    def wait(self, kind, a=0):
        for half in (0, 1):
            for d in DIRS:
                self.copy(half, kind, d, a, True).wait_recv()

    def round0(self):
        self.send("F1")
        self.send("G1", 0)

    def round1(self):
        self.wait("F1")
        self.send("F2")
        self.send("G1", 1)
        self.send("G1", 3)
        self.wait("G1", 0)
        self.send("G2", 0)
        return ((0, 0), (0, 1), (0, 3), (1, 0), (3, 0))

    def round2(self):
        self.wait("F2")
        self.send("G1", 2)
        self.wait("G1", 1)
        self.send("G2", 1)
        self.wait("G1", 3)
        self.send("G2", 3)
        self.wait("G2", 0)
        return ((1, 1), (1, 3), (3, 1), (3, 3), (2, 0), (0, 2))

    def round3(self):
        self.wait("G1", 2)
        self.send("G2", 2)
        self.wait("G2", 1)
        self.wait("G2", 3)
        return ((2, 1), (2, 3), (1, 2), (3, 2))

    def round4(self):
        self.wait("G2", 2)
        return ((2, 2),)

    def finish(self):
        whole = self.buf.at[pl.ds(0, GROUP - 1)]
        pltpu.make_async_remote_copy(
            src_ref=whole, dst_ref=whole, send_sem=self.send_sem.at[0], recv_sem=self.recv_sem.at[0],
            device_id={"dp": self.plane.slot(0, 1, 0)}, device_id_type=MESH,
        ).wait_send()


class Scatter:
    def __init__(self, plane, part, land, send_sem, recv_sem):
        self.plane, self.part, self.land = plane, part, land
        self.send_sem, self.recv_sem = send_sem, recv_sem
        self.quarter = part.shape[1] // 4

    def rows(self, half, piece):
        return pl.ds((2 * half + piece) * self.quarter, self.quarter)

    def index(self, half, kind, d, a):
        dd = 0 if d == 1 else 1
        base = {"S1": 0, "S2": 8, "S3": 16, "U1": 24, "U2": 26, "U3": 28}[kind]
        return half * 30 + base + (2 * a if kind[0] == "S" else 0) + dd

    def copy(self, half, kind, d, a):
        plane = self.plane
        dd = 0 if d == 1 else 1
        far = 2 if kind[1] == "1" else d
        piece = 1 - dd if kind[1] == "2" else dd
        if kind[0] == "S":
            q, to = plane.slot(half, a, far), plane.slot(half, 0, d)
        else:
            q, to = plane.slot(half, far, 0), plane.slot(half, d, 0)
        k = self.index(half, kind, d, a)
        return pltpu.make_async_remote_copy(
            src_ref=self.part.at[q, self.rows(half, piece)], dst_ref=self.land.at[k],
            send_sem=self.send_sem.at[0], recv_sem=self.recv_sem.at[k],
            device_id={"dp": to}, device_id_type=MESH,
        )

    def landed(self, half, kind, d, a=0):
        self.copy(half, kind, d, a).wait_recv()
        return self.land[self.index(half, kind, d, a)].astype(F32)

    def send_chunk(self, dz, dx):
        for half, a, far in ((0, dx, dz), (1, dz, dx)):
            if far == 2:
                for d in DIRS:
                    self.copy(half, "S1", d, a).start()
            elif far == 1:
                self.copy(half, "S2", 1, a).start()
            elif far == 3:
                self.copy(half, "S2", -1, a).start()

    def pass_on(self, a):
        for half in (0, 1):
            for d in DIRS:
                q, rows = self.plane.slot(half, a, d), self.rows(half, 0 if d == 1 else 1)
                total = self.part[q, rows].astype(F32) + self.landed(half, "S1", d, a)
                self.part[q, rows] = total.astype(BF16)
                self.copy(half, "S3", d, a).start()

    def settle(self, a):
        for half in (0, 1):
            q = self.plane.slot(half, a, 0)
            for piece, d in ((0, 1), (1, -1)):
                rows = self.rows(half, piece)
                total = self.part[q, rows].astype(F32) + self.landed(half, "S3", d, a) + self.landed(half, "S2", -d, a)
                self.part[q, rows] = total.astype(BF16)
            if a == 2:
                for d in DIRS:
                    self.copy(half, "U1", d, 0).start()
            elif a == 1:
                self.copy(half, "U2", 1, 0).start()
            elif a == 3:
                self.copy(half, "U2", -1, 0).start()

    def pass_last(self):
        for half in (0, 1):
            for d in DIRS:
                q, rows = self.plane.slot(half, d, 0), self.rows(half, 0 if d == 1 else 1)
                total = self.part[q, rows].astype(F32) + self.landed(half, "U1", d)
                self.part[q, rows] = total.astype(BF16)
                self.copy(half, "U3", d, 0).start()

    def result(self, total):
        me = self.plane.me
        for half in (0, 1):
            for piece, d in ((0, 1), (1, -1)):
                rows = self.rows(half, piece)
                total[rows] = (
                    self.part[me, rows].astype(F32) + self.landed(half, "U3", d) + self.landed(half, "U2", -d)
                )

    def finish(self):
        whole = self.part.at[pl.ds(0, GROUP - 1)]
        pltpu.make_async_remote_copy(
            src_ref=whole, dst_ref=whole, send_sem=self.send_sem.at[0], recv_sem=self.recv_sem.at[0],
            device_id={"dp": self.plane.slot(0, 1, 0)}, device_id_type=MESH,
        ).wait_send()


class Exchange:
    def __init__(self, plane, sems):
        self.plane, self.sems = plane, sems

    def copy(self, src, dst, to):
        return pltpu.make_async_remote_copy(
            src_ref=src, dst_ref=dst, send_sem=self.sems.at[0], recv_sem=self.sems.at[1],
            device_id={"dp": to}, device_id_type=MESH,
        )

    def start(self, src, dst):
        for k in range(1, GROUP):
            to = lax.rem(self.plane.me + k, GROUP)
            self.copy(src(to), dst(k), to).start()

    def wait_recv(self, whole):
        self.copy(whole, whole, lax.rem(self.plane.me + 1, GROUP)).wait_recv()

    def wait_send(self, whole):
        self.copy(whole, whole, lax.rem(self.plane.me + 1, GROUP)).wait_send()


def whole_kernel(
    sections, scale_a, scale_b,
    h_hbm, top_hbm, w_hbm, m_hbm, v_hbm, slot_ref, ids_ref,
    w_out, m_out, v_out, blocks_out, ids_out,
    h_v, top_v, w_v, wide, m_v, v_v,
    all_a, all_b, part_a, part_b, land_a, land_b,
    rows_a, cross_all, cross_part, cross_land, mixed_part, mixed_land, mixed,
    acc, out_t, out_n, u_all, u_acc, deltas, total, relayed, tiles, outbox, w_new, ids_in,
    local_sem, ga_send, ga_recv, gb_send, gb_recv, sa_send, sa_recv, sb_send, sb_recv,
    row_send, row_recv, cross_send, cross_recv, u_send, u_recv, swap_sem,
):
    s = lax.axis_index("section")
    plane = Plane()
    me = plane.me
    width = w_v.shape[0] // 2
    chunk = cross_part.shape[0] // GROUP
    rank = rows_a.shape[2]

    loads = [
        pltpu.make_async_copy(src, dst, local_sem.at[k])
        for k, (src, dst) in enumerate(((w_hbm, w_v), (h_hbm, h_v), (top_hbm, top_v), (m_hbm, m_v), (v_hbm, v_v)))
    ]
    for load in loads:
        load.start()

    barrier = pltpu.get_barrier_semaphore()
    for k in range(1, GROUP):
        pl.semaphore_signal(barrier, inc=1, device_id={"dp": lax.rem(me + k, GROUP)}, device_id_type=MESH)
    for k in range(1, sections):
        pl.semaphore_signal(barrier, inc=1, device_id={"section": lax.rem(s + k, sections)}, device_id_type=MESH)

    loads[0].wait()
    wide[...] = w_v[...].astype(F32)
    all_a[me] = wide[pl.ds(0, width, stride=2), :].astype(BF16)
    own_b = wide[pl.ds(1, width, stride=2), :]
    all_b[me] = own_b.astype(BF16)
    pl.semaphore_wait(barrier, GROUP - 1 + sections - 1)

    gather_a = Gather(plane, all_a, ga_send, ga_recv)
    gather_b = Gather(plane, all_b, gb_send, gb_recv)
    scatter_a = Scatter(plane, part_a, land_a, sa_send, sa_recv)
    scatter_b = Scatter(plane, part_b, land_b, sb_send, sb_recv)
    swap_cross = Exchange(plane, swap_sem.at[0])
    spread_cross = Exchange(plane, swap_sem.at[1])
    swap_mixed = Exchange(plane, swap_sem.at[2])
    spread_mixed = Exchange(plane, swap_sem.at[3])
    swap_ids = Exchange(plane, swap_sem.at[4])
    swap_tiles = Exchange(plane, swap_sem.at[5])

    def down(src, dst, send_sem, recv_sem, to):
        return pltpu.make_async_remote_copy(
            src_ref=src, dst_ref=dst, send_sem=send_sem, recv_sem=recv_sem,
            device_id={"section": to}, device_id_type=MESH,
        )

    def send_down(src, dst, send_sems, recv_sems):
        for to in range(sections - 2, -1, -1):
            @pl.when(to < s)
            def _():
                down(src, dst, send_sems.at[to], recv_sems.at[s], to).start()

    def sent_down(src, dst, send_sems, recv_sems):
        for to in range(sections - 2, -1, -1):
            @pl.when(to < s)
            def _():
                down(src, dst, send_sems.at[to], recv_sems.at[s], to).wait_send()

    def wait_above(block, send_sems, recv_sems):
        for layer in range(sections - 1, 0, -1):
            @pl.when(layer > s)
            def _():
                down(block(layer), block(layer), send_sems.at[layer], recv_sems.at[layer], layer).wait_recv()

    gather_a.round0()
    row_args = (all_a.at[me], rows_a.at[s], row_send, row_recv)
    send_down(*row_args)
    swap_ids.start(lambda q: ids_ref.at[q], lambda k: ids_in.at[me])
    ids_in[me] = ids_ref[me]
    for layer in range(sections):
        @pl.when(layer <= s)
        def _():
            rows_a[layer] = jnp.zeros(rows_a.shape[1:], BF16)
    own_bt = own_b.T.astype(BF16)

    gather_a.round1()

    wait_above(lambda layer: rows_a.at[layer], row_send, row_recv)
    for layer in range(sections):
        cross_part[layer * rank:(layer + 1) * rank] = jnp.dot(
            own_bt, rows_a[layer], preferred_element_type=F32
        ).astype(BF16)

    def piece(ref, q):
        return ref.at[pl.ds(pl.multiple_of(q * chunk, chunk), chunk)]

    swap_cross.start(lambda q: piece(cross_part, q), lambda k: cross_land.at[k - 1])
    gather_a.round2()
    gather_b.round0()
    gather_a.round3()

    swap_cross.wait_recv(cross_land)
    own_rows = pl.ds(pl.multiple_of(me * chunk, chunk), chunk)
    cross_sum = cross_part[own_rows].astype(F32)
    for k in range(GROUP - 1):
        cross_sum = cross_sum + cross_land[k].astype(F32)
    cross_all[s, own_rows] = (cross_sum * (scale_a * scale_b)).astype(BF16)
    spread_cross.start(lambda q: cross_all.at[s, own_rows], lambda k: cross_all.at[s, own_rows])

    gather_a.round4()
    loads[1].wait()

    def forward(left, blocks, q):
        cols = pl.ds(pl.multiple_of(q * width, width), width)
        return jnp.dot(left[:, cols], blocks[q], preferred_element_type=F32)

    acc[...] = jnp.zeros_like(acc)

    def forward_a(q, carry):
        acc[...] += forward(h_v, all_a, q)
        return carry

    lax.fori_loop(0, GROUP // 2, forward_a, 0)
    spots = gather_b.round1()
    lax.fori_loop(GROUP // 2, GROUP, forward_a, 0)
    adapter_out = acc[...] * scale_a
    out_n[...] = adapter_out.astype(BF16)
    out_t[...] = adapter_out.T.astype(BF16)
    loads[2].wait()

    spread_cross.wait_recv(cross_all.at[s, pl.ds(0, (GROUP - 1) * chunk)])
    cross_args = (cross_all.at[s], cross_all.at[s], cross_send, cross_recv)
    send_down(*cross_args)

    def backward(left, right, part, q):
        cols = pl.ds(pl.multiple_of(q * width, width), width)
        part[q] = jnp.dot(left, right[:, cols], preferred_element_type=F32).astype(BF16)

    def backward_b(q, carry):
        backward(out_t[...], top_v, part_b, q)
        return carry

    acc[...] = jnp.zeros_like(acc)

    def forward_b(spots):
        for dz, dx in spots:
            acc[...] += forward(top_v, all_b, plane.away(dz, dx))

    lax.fori_loop(0, GROUP // 2, backward_b, 0)
    forward_b(spots)
    spots = gather_b.round2()
    lax.fori_loop(GROUP // 2, GROUP, backward_b, 0)
    forward_b(spots)
    spots = gather_b.round3()
    order = [(2, 2)] + [(2, k) for k in (0, 1, 3)] + [(k, 2) for k in (0, 1, 3)]
    order += [(1, 1), (1, 3), (3, 1), (3, 3), (1, 0), (3, 0), (0, 1), (0, 3), (0, 0)]
    for dz, dx in order:
        scatter_b.send_chunk(dz, dx)
    forward_b(spots)
    forward_b(gather_b.round4())

    u_all[s] = (acc[...] * scale_b).T.astype(BF16)
    u_args = (u_all.at[s], u_all.at[s], u_send, u_recv)
    send_down(*u_args)
    wait_above(lambda layer: cross_all.at[layer], cross_send, cross_recv)
    wait_above(lambda layer: u_all.at[layer], u_send, u_recv)
    for layer in range(sections):
        @pl.when(layer >= s)
        def _():
            u_acc[layer] = u_all[layer].astype(F32)
    for layer in range(sections - 1, -1, -1):
        @pl.when(layer >= s)
        def _():
            delta = u_acc[layer].astype(BF16)
            deltas[layer] = delta
            for lower in range(layer):
                @pl.when(lower >= s)
                def _():
                    u_acc[lower] += jnp.dot(
                        cross_all[lower, layer * rank:(layer + 1) * rank], delta, preferred_element_type=F32
                    )

    for a in (2, 1, 3, 0):
        scatter_b.pass_on(a)

    for dz, dx in order:
        backward(deltas[s], h_v, part_a, plane.away(dz, dx))
        scatter_a.send_chunk(dz, dx)

    for layer in range(sections):
        @pl.when(layer > s)
        def _():
            mixed_part[layer * rank:(layer + 1) * rank] = jnp.dot(
                deltas[layer], out_n[...], preferred_element_type=F32
            ).astype(BF16)

        @pl.when(layer <= s)
        def _():
            mixed_part[layer * rank:(layer + 1) * rank] = jnp.zeros((rank, rank), BF16)
    swap_mixed.start(lambda q: piece(mixed_part, q), lambda k: mixed_land.at[k - 1])

    for a in (2, 1, 3, 0):
        scatter_b.settle(a)
    swap_mixed.wait_recv(mixed_land)
    mixed_sum = mixed_part[own_rows].astype(F32)
    for k in range(GROUP - 1):
        mixed_sum = mixed_sum + mixed_land[k].astype(F32)
    mixed[own_rows] = mixed_sum.astype(BF16)
    spread_mixed.start(lambda q: mixed.at[own_rows], lambda k: mixed.at[own_rows])
    scatter_b.pass_last()
    for a in (2, 1, 3, 0):
        scatter_a.pass_on(a)
    spread_mixed.wait_recv(mixed.at[pl.ds(0, (GROUP - 1) * chunk)])
    loads[3].wait()
    loads[4].wait()

    def adam(which, gradient_of):
        for block in range(width // BS):
            rows = pl.ds(2 * BS * block + which, BS, stride=2)
            gradient = gradient_of(pl.ds(block * BS, BS))
            new_first = beta_one * m_v[rows, :] + (1.0 - beta_one) * gradient
            new_second = beta_two * v_v[rows, :] + (1.0 - beta_two) * gradient * gradient
            master = wide[rows, :]
            update = new_first / correct_one / (jnp.sqrt(new_second / correct_two) + adam_eps)
            fresh = master - learn_rate * (update + decay_rate * master)
            m_v[rows, :] = new_first
            v_v[rows, :] = new_second
            wide[rows, :] = fresh
            tiles[2 * block + which] = fresh.astype(BF16)

    relayed[...] = jnp.dot(rows_a[0], mixed[0:rank], preferred_element_type=F32)
    for layer in range(1, sections):
        relayed[...] += jnp.dot(
            rows_a[layer], mixed[layer * rank:(layer + 1) * rank], preferred_element_type=F32
        )
    scatter_b.result(total)
    adam(1, lambda rows: (total[:, rows].T + relayed[rows] * scale_a) * scale_b)

    for a in (2, 1, 3, 0):
        scatter_a.settle(a)
    scatter_a.pass_last()
    scatter_a.result(total)
    adam(0, lambda rows: total[:, rows].T * scale_a)

    for k in range(GROUP * CAP):
        index = slot_ref[k // 128, k % 128]
        tile = tiles[jnp.maximum(index, 0)]
        outbox[k // CAP, k % CAP] = jnp.where(index >= 0, tile, jnp.zeros_like(tile))
    swap_tiles.start(lambda q: outbox.at[q], lambda k: blocks_out.at[me])
    kept = pltpu.make_async_copy(outbox.at[me], blocks_out.at[me], local_sem.at[5])
    kept.start()
    w_new[...] = wide[...].astype(BF16)
    stores = [
        pltpu.make_async_copy(src, dst, local_sem.at[k])
        for k, (src, dst) in enumerate(((w_new, w_out), (m_v, m_out), (v_v, v_out)))
    ]
    for store in stores:
        store.start()
    swap_ids.wait_recv(ids_in.at[pl.ds(0, GROUP - 1)])
    stores.append(pltpu.make_async_copy(ids_in, ids_out, local_sem.at[3]))
    stores[-1].start()

    gather_a.finish()
    gather_b.finish()
    scatter_a.finish()
    scatter_b.finish()
    sent_down(*row_args)
    sent_down(*cross_args)
    sent_down(*u_args)
    swap_ids.wait_send(ids_ref.at[pl.ds(0, GROUP - 1)])
    swap_cross.wait_send(cross_land)
    swap_mixed.wait_send(mixed_land)
    spread_cross.wait_send(mixed.at[pl.ds(0, (GROUP - 1) * chunk)])
    spread_mixed.wait_send(mixed.at[pl.ds(0, (GROUP - 1) * chunk)])
    swap_tiles.wait_send(outbox.at[pl.ds(0, GROUP - 1)])
    swap_tiles.wait_recv(blocks_out.at[pl.ds(0, GROUP - 1)])
    kept.wait()
    for store in stores:
        store.wait()


def shards(section_inputs, top_grad, weights, first_moment, second_moment, block_list, block_owner):
    sections = lax.axis_size("section")
    model_width = section_inputs.shape[3]
    rank = weights.shape[3]
    width = weights.shape[1]
    tokens = section_inputs.shape[1] * section_inputs.shape[2]
    chunk = sections * rank // GROUP
    scale_a = model_width ** (-0.5)
    scale_b = rank ** (-0.5)

    chosen = block_list[0, 0]
    owners = block_owner[0, 0, :, 0]
    positions = jnp.arange(chosen.shape[0], dtype=jnp.int32)
    same_owner = (owners[None, :] == owners[:, None]) & (positions[None, :] < positions[:, None])
    place = jnp.sum(same_owner.astype(jnp.int32), axis=1)
    selector = (owners[None, :] * CAP + place[None, :]) == jnp.arange(GROUP * CAP, dtype=jnp.int32)[:, None]
    slots = jnp.sum(jnp.where(selector, chosen[None, :] + 1, 0), axis=1) - 1
    tile_count = width * 2 // BS
    ids = jnp.where(slots >= 0, lax.axis_index("dp") * tile_count + slots, -1)
    ids = jnp.broadcast_to(ids.reshape(GROUP, 1, CAP), (GROUP, 8, CAP))
    ids = jnp.pad(ids, ((0, 0), (0, 0), (0, 128 - CAP)))
    slots = jnp.pad(slots[None], ((0, 0), (0, 128 - GROUP * CAP)))

    any_spec = pl.BlockSpec(memory_space=pl.ANY)
    vmem = pl.BlockSpec(memory_space=pltpu.VMEM)
    dma = pltpu.SemaphoreType.DMA
    new_weights, new_first, new_second, blocks, got_ids = pl.pallas_call(
        functools.partial(whole_kernel, sections, scale_a, scale_b),
        out_shape=(
            jax.ShapeDtypeStruct((2 * width, rank), BF16),
            jax.ShapeDtypeStruct((2 * width, rank), F32),
            jax.ShapeDtypeStruct((2 * width, rank), F32),
            jax.ShapeDtypeStruct((GROUP, CAP, BS, BS), BF16),
            jax.ShapeDtypeStruct((GROUP, 8, 128), jnp.int32),
        ),
        in_specs=[any_spec] * 5 + [pl.BlockSpec(memory_space=pltpu.SMEM), vmem],
        out_specs=(any_spec,) * 5,
        scratch_shapes=[
            pltpu.VMEM((tokens, model_width), BF16),
            pltpu.VMEM((tokens, model_width), BF16),
            pltpu.VMEM((2 * width, rank), BF16),
            pltpu.VMEM((2 * width, rank), F32),
            pltpu.VMEM((2 * width, rank), F32),
            pltpu.VMEM((2 * width, rank), F32),
            pltpu.VMEM((GROUP, width, rank), BF16),
            pltpu.VMEM((GROUP, width, rank), BF16),
            pltpu.VMEM((GROUP, rank, width), BF16),
            pltpu.VMEM((GROUP, rank, width), BF16),
            pltpu.VMEM((60, rank // 4, width), BF16),
            pltpu.VMEM((60, rank // 4, width), BF16),
            pltpu.VMEM((sections, width, rank), BF16),
            pltpu.VMEM((sections, sections * rank, rank), BF16),
            pltpu.VMEM((sections * rank, rank), BF16),
            pltpu.VMEM((GROUP - 1, chunk, rank), BF16),
            pltpu.VMEM((sections * rank, rank), BF16),
            pltpu.VMEM((GROUP - 1, chunk, rank), BF16),
            pltpu.VMEM((sections * rank, rank), BF16),
            pltpu.VMEM((tokens, rank), F32),
            pltpu.VMEM((rank, tokens), BF16),
            pltpu.VMEM((tokens, rank), BF16),
            pltpu.VMEM((sections, rank, tokens), BF16),
            pltpu.VMEM((sections, rank, tokens), F32),
            pltpu.VMEM((sections, rank, tokens), BF16),
            pltpu.VMEM((rank, width), F32),
            pltpu.VMEM((width, rank), F32),
            pltpu.VMEM((2 * width // BS, BS, BS), BF16),
            pltpu.VMEM((GROUP, CAP, BS, BS), BF16),
            pltpu.VMEM((2 * width, rank), BF16),
            pltpu.VMEM((GROUP, 8, 128), jnp.int32),
            dma((6,)),
            dma((1,)), dma((40,)), dma((1,)), dma((40,)),
            dma((1,)), dma((60,)), dma((1,)), dma((60,)),
            dma((sections,)), dma((sections,)),
            dma((sections,)), dma((sections,)),
            dma((sections,)), dma((sections,)),
            dma((6, 2)),
        ],
        compiler_params=pltpu.CompilerParams(
            collective_id=0, has_side_effects=True, vmem_limit_bytes=62 * 1024 * 1024
        ),
        cost_estimate=pl.CostEstimate(
            flops=8 * tokens * model_width * rank, bytes_accessed=4 * tokens * model_width, transcendentals=0
        ),
    )(
        section_inputs.reshape(tokens, model_width),
        top_grad.reshape(tokens, model_width),
        weights.reshape(2 * width, rank),
        first_moment.reshape(2 * width, rank),
        second_moment.reshape(2 * width, rank),
        slots,
        ids,
    )
    return (
        new_weights.reshape(weights.shape),
        new_first.reshape(weights.shape),
        new_second.reshape(weights.shape),
        blocks[None, None],
        got_ids[:, 0, :CAP][None, None],
    )


def solution(mesh):
    placed = (
        P("section", None, "dp", None),
        P(None, "dp", None),
        P("section", "dp", None, None),
        P("section", "dp", None, None),
        P("section", "dp", None, None),
        P("section", "dp", None),
        P("section", "dp", None, None),
    )
    return jax.shard_map(
        shards,
        mesh=mesh,
        in_specs=placed,
        out_specs=(
            P("section", "dp", None, None),
            P("section", "dp", None, None),
            P("section", "dp", None, None),
            P("section", "dp", None, None, None, None),
            P("section", "dp", None, None),
        ),
        check_vma=False,
    )
```

time: 496 us -> 150 us (0.30)
  waiting for transfers between devices: 288 us -> 0 us
  Pallas kernels: 0 us -> 135 us
  blocking collectives: 82 us -> 0 us
  matrix products: 61 us -> 0 us
  local copies, waits for them, and re-layouts: 26.2 us -> 11.7 us
  between operations: 14.6 us -> 0.66 us
  starting transfers between devices: 12.4 us -> 0 us
  other arithmetic: 8.89 us -> 2.33 us
    all_gather x5 -> x0, waiting for transfers between devices: 165 us -> none  [the longest x1 51.9 us: shards(): adapt_b = lax.all_gather(rows_b, 'dp', axis=0, tiled=True)]
    pallas_call x0 -> x1, Pallas kernels: none -> 135 us  [shards(): pl.pallas_call(functools.partial(whole_kernel, sections, scale_a, scale_b...]
    psum x1 -> x0, waiting for transfers between devices: 85 us -> none  [shards(): lax.psum(lax.dot_general(every_a, rows_b, (((1,), (0,)), ((), ())), prefe...]
    psum x1 -> x0, blocking collectives: 82 us -> none  [shards(): lax.psum(lax.dot_general(deltas, adapter_out, (((1,), (0,)), ((), ())), p...]
    dot_general x36 -> x0, matrix products: 61 us -> none  [the longest x28 26.3 us: shards(): jnp.dot(deltas[upper], every_cross[layer, upper], preferred_element_type=...]
    reduce_scatter x2 -> x0, waiting for transfers between devices: 26 us -> none  [the longest x1 26 us: shards(): lax.psum_scatter(part_a, 'dp', scatter_dimension=0, tiled=True)]
    all_to_all x2 -> x0, starting transfers between devices: 12.1 us -> none  [the longest x1 7.02 us: shards(): lax.all_to_all(send_ids, 'dp', split_axis=0, concat_axis=0, tiled=True)]
    all_to_all x2 -> x0, waiting for transfers between devices: 10.7 us -> none  [the longest x1 10.7 us: shards(): lax.all_to_all(send_tiles, 'dp', split_axis=0, concat_axis=0, tiled=True)]
  transfers between devices with their start and end apart: 10 -> 0, of which waited for: 8 -> 0; matrix products, arithmetic and copies ran while one was open for 18% -> 0% of each run, Pallas kernels for 0% -> 0%
where the time goes in v2:
time: 150 us
  Pallas kernels  135 us (90%)
  local copies, waits for them, and re-layouts  11.7 us (8%)
  other arithmetic  2.33 us (2%)
    pallas_call x1, Pallas kernels, shards(): pl.pallas_call(functools.partial(whole_kernel, sections, scale_a, scale_b...  135 us
    unnamed x4, local copies, waits for them, and re-layouts  9.02 us

profile of v2, /device:TPU:0, one launch (start us, length us, event | category | flops | bytes accessed | tf_op | source)
XLA Modules:
  0.0 149.9 jit_solution(8802410174223778267)
XLA Ops:
  0.6 0.7 add_bitcast_fusion
  1.3 0.9 convert_reduce_fusion
  2.2 0.7 multiply_add_fusion
  2.9 0.1 select_reduce_fusion
  3.0 0.5 pad.8.slot_ref
  3.5 0.1 select_n.17
  3.6 0.6 pad.9.ids_ref
  4.2 135.2 %shard_map.110 = (bf16[2048,128]{1,0:T(8,128)(2,1)}, f32[2048,128]{1,0:T(8,128)}, f32[2048,128]{1,0:T(8,128)}, bf16[16,2,128,128]{3,2,1,0:T(8,128)(2,1)}, s32[16,8,128]{2,1,0:T(8,128)}) custom-call(bf16[256,16384]{1,0:T(8,128)(2,1)} %bitcast.16, bf16[256,16384]{1,0:T(8,128)(2,1)} %bitcast.17, bf16[2048,128]{1,0:T(8,128)(2,1)} %bitcast.23, ...), custom_call_target="tpu_custom_call" | custom-call | flops 4294967296 | bytes 16777216 | tf_op jit(solution)/shard_map/pallas_call | solution.py:551
  139.4 0.8 slice.3
  140.3 0.6 copy.14
  140.9 2.2 %copy.19 = bf16[1,1024,2,128]{3,2,1,0:T(2,128)(2,1)} copy(bf16[1,1024,2,128]{3,2,1,0:T(2,128)(2,1)} %bitcast.24) | data formatting | bytes 1048576
  143.1 2.3 %copy.20 = f32[1,1024,2,128]{3,2,1,0:T(2,128)} copy(f32[1,1024,2,128]{3,2,1,0:T(2,128)} %bitcast.22) | data formatting | bytes 2097152
  145.4 2.3 %copy.21 = f32[1,1024,2,128]{3,2,1,0:T(2,128)} copy(f32[1,1024,2,128]{3,2,1,0:T(2,128)} %bitcast.21) | data formatting | bytes 2097152
  147.6 2.3 %copy.22 = bf16[1,1,16,2,128,128]{5,4,3,2,1,0:T(8,128)(2,1)} copy(bf16[1,1,16,2,128,128]{5,4,3,2,1,0:T(8,128)(2,1)} %bitcast.20) | data formatting | bytes 2097152
  (2 shorter events, 0.0 us)

commit v3 on v2

--- a/solution.py
+++ b/solution.py
@@ -220,6 +220,70 @@
         ).wait_send()
 
 
+class Ring:
+    def __init__(self, plane, buf, land, send_sem, recv_sem):
+        self.plane, self.buf, self.land, self.send_sem, self.recv_sem = plane, buf, land, send_sem, recv_sem
+        self.z = plane.place[1][0]
+        self.half = buf.shape[1] // 2
+
+    def piece(self, which):
+        return pl.ds(which * self.half, self.half)
+
+    def copy(self, src, dst, k, d):
+        return pltpu.make_async_remote_copy(
+            src_ref=src, dst_ref=dst, send_sem=self.send_sem.at[0], recv_sem=self.recv_sem.at[k],
+            device_id={"dp": self.plane.slot(0, 0, d)}, device_id_type=MESH,
+        )
+
+    def gather_copy(self, kind, d, arriving):
+        dd = 0 if d == 1 else 1
+        hop = -d if arriving else 0
+        if kind == 1:
+            where = self.buf.at[wrap(self.z + hop)]
+        else:
+            where = self.buf.at[wrap(self.z + hop - d), self.piece(dd)]
+        return self.copy(where, where, 2 * (kind - 1) + dd, d)
+
+    def gather_send(self, kind):
+        for d in DIRS:
+            self.gather_copy(kind, d, False).start()
+
+    def gather_wait(self, kind):
+        for d in DIRS:
+            self.gather_copy(kind, d, True).wait_recv()
+
+    def sum_copy(self, kind, d):
+        dd = 0 if d == 1 else 1
+        far = 2 if kind == 1 else d
+        k = 2 * (kind - 1) + dd
+        src = self.buf.at[wrap(self.z + far), self.piece(1 - dd if kind == 2 else dd)]
+        return self.copy(src, self.land.at[k], k, d)
+
+    def landed(self, kind, d):
+        self.sum_copy(kind, d).wait_recv()
+        return self.land[2 * (kind - 1) + (0 if d == 1 else 1)].astype(F32)
+
+    def sum_send(self):
+        for kind in (1, 2):
+            for d in DIRS:
+                self.sum_copy(kind, d).start()
+
+    def sum_pass(self):
+        for d in DIRS:
+            spot, rows = wrap(self.z + d), self.piece(0 if d == 1 else 1)
+            self.buf[spot, rows] = (self.buf[spot, rows].astype(F32) + self.landed(1, d)).astype(BF16)
+            self.sum_copy(3, d).start()
+
+    def sum_result(self, total):
+        for which, d in ((0, 1), (1, -1)):
+            rows = self.piece(which)
+            total[rows] = self.buf[self.z, rows].astype(F32) + self.landed(3, d) + self.landed(2, -d)
+
+    def finish(self):
+        whole = self.buf.at[pl.ds(0, RING - 1)]
+        self.copy(whole, whole, 0, 1).wait_send()
+
+
 class Exchange:
     def __init__(self, plane, sems):
         self.plane, self.sems = plane, sems
@@ -244,14 +308,14 @@
 
 def whole_kernel(
     sections, scale_a, scale_b,
-    h_hbm, top_hbm, w_hbm, m_hbm, v_hbm, slot_ref, ids_ref,
+    h_hbm, top_hbm, w_hbm, m_hbm, v_hbm, list_ref, owner_ref,
     w_out, m_out, v_out, blocks_out, ids_out,
-    h_v, top_v, w_v, wide, m_v, v_v,
-    all_a, all_b, part_a, part_b, land_a, land_b,
+    h_v, w_v, wide, m_v, v_v,
+    all_a, part_a, land_a, ring_b, slice_b, merged, u_part, u_land, u_turn, u_near, outs, grad_out, part_b, land_b,
     rows_a, cross_all, cross_part, cross_land, mixed_part, mixed_land, mixed,
-    acc, out_t, out_n, u_all, u_acc, deltas, total, relayed, tiles, outbox, w_new, ids_in,
+    acc, out_n, u_all, u_acc, deltas, total, relayed, tiles, outbox, w_new, ids_in, ids_ref, slot_ref,
     local_sem, ga_send, ga_recv, gb_send, gb_recv, sa_send, sa_recv, sb_send, sb_recv,
-    row_send, row_recv, cross_send, cross_recv, u_send, u_recv, swap_sem,
+    row_send, row_turn, row_recv, cross_send, cross_recv, u_send, u_turn_sem, u_recv, swap_sem, near_sem,
 ):
     s = lax.axis_index("section")
     plane = Plane()
@@ -259,11 +323,17 @@
     width = w_v.shape[0] // 2
     chunk = cross_part.shape[0] // GROUP
     rank = rows_a.shape[2]
+    level, core = s // 2, lax.rem(s, 2)
+    x = plane.place[0][0]
+    tokens = h_v.shape[0]
+    half_cols = pl.ds(pl.multiple_of(core * (width // 2), width // 2), width // 2)
 
     loads = [
         pltpu.make_async_copy(src, dst, local_sem.at[k])
-        for k, (src, dst) in enumerate(((w_hbm, w_v), (h_hbm, h_v), (top_hbm, top_v), (m_hbm, m_v), (v_hbm, v_v)))
+        for k, (src, dst) in enumerate(((w_hbm, w_v), (h_hbm, h_v), (m_hbm, m_v), (v_hbm, v_v)))
     ]
+    own_cols = pl.ds(pl.multiple_of((level * RING + x) * width, width), width)
+    loads.append(pltpu.make_async_copy(top_hbm.at[:, own_cols], merged.at[x], local_sem.at[4]))
     for load in loads:
         load.start()
 
@@ -277,13 +347,13 @@
     wide[...] = w_v[...].astype(F32)
     all_a[me] = wide[pl.ds(0, width, stride=2), :].astype(BF16)
     own_b = wide[pl.ds(1, width, stride=2), :]
-    all_b[me] = own_b.astype(BF16)
+    ring_b[plane.place[1][0]] = own_b.astype(BF16)
     pl.semaphore_wait(barrier, GROUP - 1 + sections - 1)
 
     gather_a = Gather(plane, all_a, ga_send, ga_recv)
-    gather_b = Gather(plane, all_b, gb_send, gb_recv)
+    ring_gather = Ring(plane, ring_b, None, gb_send, gb_recv)
     scatter_a = Scatter(plane, part_a, land_a, sa_send, sa_recv)
-    scatter_b = Scatter(plane, part_b, land_b, sb_send, sb_recv)
+    ring_sum = Ring(plane, part_b, land_b, sb_send, sb_recv)
     swap_cross = Exchange(plane, swap_sem.at[0])
     spread_cross = Exchange(plane, swap_sem.at[1])
     swap_mixed = Exchange(plane, swap_sem.at[2])
@@ -297,27 +367,127 @@
             device_id={"section": to}, device_id_type=MESH,
         )
 
-    def send_down(src, dst, send_sems, recv_sems):
-        for to in range(sections - 2, -1, -1):
-            @pl.when(to < s)
+    def send_cross(waiting):
+        for layer in range(1, sections - 1):
+            @pl.when(s == layer)
             def _():
-                down(src, dst, send_sems.at[to], recv_sems.at[s], to).start()
-
-    def sent_down(src, dst, send_sems, recv_sems):
-        for to in range(sections - 2, -1, -1):
-            @pl.when(to < s)
-            def _():
-                down(src, dst, send_sems.at[to], recv_sems.at[s], to).wait_send()
-
-    def wait_above(block, send_sems, recv_sems):
-        for layer in range(sections - 1, 0, -1):
+                block = cross_all.at[layer, pl.ds((layer + 1) * rank, (sections - 1 - layer) * rank)]
+                for to in range(layer - 1, -1, -1):
+                    copy = down(block, block, cross_send.at[to], cross_recv.at[layer], to)
+                    if waiting:
+                        copy.wait_send()
+                    else:
+                        copy.start()
+
+    def wait_cross():
+        for layer in range(1, sections - 1):
             @pl.when(layer > s)
             def _():
-                down(block(layer), block(layer), send_sems.at[layer], recv_sems.at[layer], layer).wait_recv()
-
+                block = cross_all.at[layer, pl.ds((layer + 1) * rank, (sections - 1 - layer) * rank)]
+                down(block, block, cross_send.at[layer], cross_recv.at[layer], layer).wait_recv()
+
+    class Cascade:
+        def __init__(self, blocks, send_sem, turn_sem, recv_sem):
+            self.blocks, self.send_sem, self.turn_sem, self.recv_sem = blocks, send_sem, turn_sem, recv_sem
+
+        def copy(self, src, layer, sem, to):
+            return down(src, self.blocks.at[layer], sem, self.recv_sem.at[layer], to)
+
+        def outgoing(self, src, act):
+            for to in range(sections // 2 - 2, -1, -1):
+                @pl.when(to < level)
+                def _():
+                    act(self.copy(src, s, self.send_sem.at[to], 2 * to + core))
+
+            @pl.when(core == 1)
+            def _():
+                act(self.copy(src, s, self.send_sem.at[RING - 1], s - 1))
+
+        def send(self, src):
+            self.outgoing(src, lambda copy: copy.start())
+
+        def relay(self):
+            for layer in range(sections - 1, 1, -1):
+                @pl.when((layer // 2 > level) & (core == layer % 2))
+                def _():
+                    block = self.blocks.at[layer]
+                    self.copy(block, layer, self.turn_sem.at[layer], s + 1 - 2 * core).wait_recv()
+                    self.copy(block, layer, self.turn_sem.at[layer], s + 1 - 2 * core).start()
+
+        def rest(self):
+            for layer in range(sections - 1, 0, -1):
+                @pl.when((layer > s) & ((layer // 2 == level) | (core != layer % 2)))
+                def _():
+                    block = self.blocks.at[layer]
+                    self.copy(block, layer, self.turn_sem.at[layer], s + 1 - 2 * core).wait_recv()
+
+        def finish(self, src):
+            self.outgoing(src, lambda copy: copy.wait_send())
+            for layer in range(sections - 1, 1, -1):
+                @pl.when((layer // 2 > level) & (core == layer % 2))
+                def _():
+                    self.copy(self.blocks.at[layer], layer, self.turn_sem.at[layer], s + 1 - 2 * core).wait_send()
+
+    row_cascade = Cascade(rows_a, row_send, row_turn, row_recv)
+    u_cascade = Cascade(u_all, u_send, u_turn_sem, u_recv)
+
+    def near(src, dst, group, k):
+        to = plane.slot(0, k, 0)
+        return pltpu.make_async_remote_copy(
+            src_ref=src, dst_ref=dst, send_sem=near_sem.at[group, 0], recv_sem=near_sem.at[group, k],
+            device_id={"dp": to}, device_id_type=MESH,
+        )
+
+    def across(src, dst, group, k):
+        to = wrap(level + k) * 2 + core
+        return pltpu.make_async_remote_copy(
+            src_ref=src, dst_ref=dst, send_sem=near_sem.at[group, 0], recv_sem=near_sem.at[group, k],
+            device_id={"section": to}, device_id_type=MESH,
+        )
+
+    def twin(src, dst, group, k):
+        return pltpu.make_async_remote_copy(
+            src_ref=src, dst_ref=dst, send_sem=near_sem.at[group, 0], recv_sem=near_sem.at[group, k],
+            device_id={"section": s + 1 - 2 * core}, device_id_type=MESH,
+        )
+
+    HOPS = (1, 3, 2)
+
+    def top_copy(k):
+        cols = pl.ds(
+            pl.multiple_of((level * RING + wrap(x + k)) * width + core * (width // 2), width // 2), width // 2
+        )
+        return near(top_hbm.at[:, cols], merged.at[x, :, half_cols], 0, k)
+
+    ring_gather.gather_send(1)
+    for k in HOPS:
+        top_copy(k).start()
     gather_a.round0()
-    row_args = (all_a.at[me], rows_a.at[s], row_send, row_recv)
-    send_down(*row_args)
+    row_cascade.send(all_a.at[me])
+
+    entries = list_ref.shape[1]
+    chosen = [list_ref[0, i] for i in range(entries)]
+    owners = [owner_ref[0, i] for i in range(entries)]
+    keys = []
+    for i in range(entries):
+        place = jnp.int32(0)
+        for j in range(i):
+            place += (owners[j] == owners[i]).astype(jnp.int32)
+        keys.append(owners[i] * CAP + place)
+    lane = lax.broadcasted_iota(jnp.int32, ids_ref.shape[1:], 1)
+
+    def fill_slot(owner, carry):
+        row = jnp.full(ids_ref.shape[1:], -1, jnp.int32)
+        for place in range(CAP):
+            index = jnp.int32(-1)
+            for i in range(entries):
+                index = jnp.where(keys[i] == owner * CAP + place, chosen[i], index)
+            slot_ref[owner * CAP + place] = index
+            row = jnp.where(lane == place, jnp.where(index >= 0, me * tiles.shape[0] + index, -1), row)
+        ids_ref[owner] = row
+        return carry
+
+    lax.fori_loop(0, GROUP, fill_slot, 0)
     swap_ids.start(lambda q: ids_ref.at[q], lambda k: ids_in.at[me])
     ids_in[me] = ids_ref[me]
     for layer in range(sections):
@@ -326,9 +496,25 @@
             rows_a[layer] = jnp.zeros(rows_a.shape[1:], BF16)
     own_bt = own_b.T.astype(BF16)
 
+    ring_gather.gather_wait(1)
+    ring_gather.gather_send(2)
     gather_a.round1()
 
-    wait_above(lambda layer: rows_a.at[layer], row_send, row_recv)
+    def passed_on(k):
+        spot = merged.at[wrap(x - k), :, half_cols]
+        return twin(spot, spot, 1, k)
+
+    for k in HOPS:
+        spot = merged.at[wrap(x - k), :, half_cols]
+        near(spot, spot, 0, k).wait_recv()
+        passed_on(k).start()
+    ring_gather.gather_wait(2)
+    for k in HOPS:
+        across(ring_b.at[wrap(level + k)], slice_b.at[level], 2, k).start()
+    slice_b[level] = ring_b[level]
+
+    row_cascade.relay()
+    row_cascade.rest()
     for layer in range(sections):
         cross_part[layer * rank:(layer + 1) * rank] = jnp.dot(
             own_bt, rows_a[layer], preferred_element_type=F32
@@ -339,7 +525,22 @@
 
     swap_cross.start(lambda q: piece(cross_part, q), lambda k: cross_land.at[k - 1])
     gather_a.round2()
-    gather_b.round0()
+
+    loads[4].wait()
+    other_cols = pl.ds(pl.multiple_of((1 - core) * (width // 2), width // 2), width // 2)
+    for k in HOPS:
+        spot = merged.at[wrap(x - k), :, other_cols]
+        twin(spot, spot, 1, k).wait_recv()
+
+    def direct(layer_level, dst):
+        for spot in range(RING):
+            dst[spot] = jnp.dot(merged[spot], slice_b[layer_level], preferred_element_type=F32).astype(BF16)
+
+    for n, k in enumerate(HOPS):
+        across(slice_b.at[wrap(level - k)], slice_b.at[wrap(level - k)], 2, k).wait_recv()
+        direct(wrap(level - k), u_part.at[n])
+        across(u_part.at[n], u_land.at[n], 3, RING - k).start()
+    direct(level, u_part.at[RING - 1])
     gather_a.round3()
 
     swap_cross.wait_recv(cross_land)
@@ -364,49 +565,53 @@
         return carry
 
     lax.fori_loop(0, GROUP // 2, forward_a, 0)
-    spots = gather_b.round1()
+
+    for n, k in enumerate(HOPS):
+        across(u_part.at[n], u_land.at[n], 3, RING - k).wait_recv()
+
+    def turn(spot):
+        summed = u_part[RING - 1, spot].astype(F32)
+        for n in range(RING - 1):
+            summed = summed + u_land[n, spot].astype(F32)
+        return summed
+
+    def u_copy(k):
+        return near(u_turn.at[k - 1], u_near.at[k - 1], 4, k)
+
+    for k in HOPS:
+        u_turn[k - 1] = turn(wrap(x + k)).astype(BF16)
+        u_copy(k).start()
     lax.fori_loop(GROUP // 2, GROUP, forward_a, 0)
     adapter_out = acc[...] * scale_a
     out_n[...] = adapter_out.astype(BF16)
-    out_t[...] = adapter_out.T.astype(BF16)
-    loads[2].wait()
+    outs[level, x] = adapter_out.T.astype(BF16)
+    for k in HOPS:
+        near(outs.at[level, x], outs.at[level, x], 5, k).start()
 
     spread_cross.wait_recv(cross_all.at[s, pl.ds(0, (GROUP - 1) * chunk)])
-    cross_args = (cross_all.at[s], cross_all.at[s], cross_send, cross_recv)
-    send_down(*cross_args)
+    send_cross(False)
 
     def backward(left, right, part, q):
         cols = pl.ds(pl.multiple_of(q * width, width), width)
         part[q] = jnp.dot(left, right[:, cols], preferred_element_type=F32).astype(BF16)
 
-    def backward_b(q, carry):
-        backward(out_t[...], top_v, part_b, q)
-        return carry
-
-    acc[...] = jnp.zeros_like(acc)
-
-    def forward_b(spots):
-        for dz, dx in spots:
-            acc[...] += forward(top_v, all_b, plane.away(dz, dx))
-
-    lax.fori_loop(0, GROUP // 2, backward_b, 0)
-    forward_b(spots)
-    spots = gather_b.round2()
-    lax.fori_loop(GROUP // 2, GROUP, backward_b, 0)
-    forward_b(spots)
-    spots = gather_b.round3()
     order = [(2, 2)] + [(2, k) for k in (0, 1, 3)] + [(k, 2) for k in (0, 1, 3)]
     order += [(1, 1), (1, 3), (3, 1), (3, 3), (1, 0), (3, 0), (0, 1), (0, 3), (0, 0)]
-    for dz, dx in order:
-        scatter_b.send_chunk(dz, dx)
-    forward_b(spots)
-    forward_b(gather_b.round4())
-
-    u_all[s] = (acc[...] * scale_b).T.astype(BF16)
-    u_args = (u_all.at[s], u_all.at[s], u_send, u_recv)
-    send_down(*u_args)
-    wait_above(lambda layer: cross_all.at[layer], cross_send, cross_recv)
-    wait_above(lambda layer: u_all.at[layer], u_send, u_recv)
+    own_direct = turn(x)
+    for k in HOPS:
+        u_copy(k).wait_recv()
+        own_direct = own_direct + u_near[k - 1].astype(F32)
+
+    u_all[s] = (own_direct * scale_b).T.astype(BF16)
+    u_cascade.send(u_all.at[s])
+    for k in HOPS:
+        spot = outs.at[level, wrap(x - k)]
+        near(spot, spot, 5, k).wait_recv()
+    for k in HOPS:
+        across(outs.at[level], outs.at[level], 6, k).start()
+    wait_cross()
+    u_cascade.relay()
+    u_cascade.rest()
     for layer in range(sections):
         @pl.when(layer >= s)
         def _():
@@ -423,9 +628,6 @@
                         cross_all[lower, layer * rank:(layer + 1) * rank], delta, preferred_element_type=F32
                     )
 
-    for a in (2, 1, 3, 0):
-        scatter_b.pass_on(a)
-
     for dz, dx in order:
         backward(deltas[s], h_v, part_a, plane.away(dz, dx))
         scatter_a.send_chunk(dz, dx)
@@ -442,20 +644,37 @@
             mixed_part[layer * rank:(layer + 1) * rank] = jnp.zeros((rank, rank), BF16)
     swap_mixed.start(lambda q: piece(mixed_part, q), lambda k: mixed_land.at[k - 1])
 
-    for a in (2, 1, 3, 0):
-        scatter_b.settle(a)
+    def top_grad_of(layer_level):
+        summed = jnp.dot(outs[layer_level, 0], merged[0], preferred_element_type=F32)
+        for spot in range(1, RING):
+            summed = summed + jnp.dot(outs[layer_level, spot], merged[spot], preferred_element_type=F32)
+        return summed.astype(BF16)
+
+    for n, k in enumerate(HOPS):
+        spot = outs.at[wrap(level - k)]
+        across(spot, spot, 6, k).wait_recv()
+        grad_out[n] = top_grad_of(wrap(level - k))
+        across(grad_out.at[n], part_b.at[level], 7, RING - k).start()
+    part_b[level] = top_grad_of(level)
     swap_mixed.wait_recv(mixed_land)
     mixed_sum = mixed_part[own_rows].astype(F32)
     for k in range(GROUP - 1):
         mixed_sum = mixed_sum + mixed_land[k].astype(F32)
     mixed[own_rows] = mixed_sum.astype(BF16)
     spread_mixed.start(lambda q: mixed.at[own_rows], lambda k: mixed.at[own_rows])
-    scatter_b.pass_last()
     for a in (2, 1, 3, 0):
         scatter_a.pass_on(a)
+    for k in HOPS:
+        spot = part_b.at[wrap(level - k)]
+        across(spot, spot, 7, k).wait_recv()
+    ring_sum.sum_send()
+    for a in (2, 1, 3, 0):
+        scatter_a.settle(a)
+    ring_sum.sum_pass()
+    scatter_a.pass_last()
     spread_mixed.wait_recv(mixed.at[pl.ds(0, (GROUP - 1) * chunk)])
+    loads[2].wait()
     loads[3].wait()
-    loads[4].wait()
 
     def adam(which, gradient_of):
         for block in range(width // BS):
@@ -476,17 +695,14 @@
         relayed[...] += jnp.dot(
             rows_a[layer], mixed[layer * rank:(layer + 1) * rank], preferred_element_type=F32
         )
-    scatter_b.result(total)
+    ring_sum.sum_result(total)
     adam(1, lambda rows: (total[:, rows].T + relayed[rows] * scale_a) * scale_b)
 
-    for a in (2, 1, 3, 0):
-        scatter_a.settle(a)
-    scatter_a.pass_last()
     scatter_a.result(total)
     adam(0, lambda rows: total[:, rows].T * scale_a)
 
     for k in range(GROUP * CAP):
-        index = slot_ref[k // 128, k % 128]
+        index = slot_ref[k]
         tile = tiles[jnp.maximum(index, 0)]
         outbox[k // CAP, k % CAP] = jnp.where(index >= 0, tile, jnp.zeros_like(tile))
     swap_tiles.start(lambda q: outbox.at[q], lambda k: blocks_out.at[me])
@@ -504,12 +720,18 @@
     stores[-1].start()
 
     gather_a.finish()
-    gather_b.finish()
+    ring_gather.finish()
     scatter_a.finish()
-    scatter_b.finish()
-    sent_down(*row_args)
-    sent_down(*cross_args)
-    sent_down(*u_args)
+    ring_sum.finish()
+    for group, whole in (
+        (0, merged.at[pl.ds(0, RING - 1), :, half_cols]), (1, merged.at[pl.ds(0, RING - 1), :, half_cols]),
+        (2, slice_b.at[pl.ds(0, RING - 1)]), (3, u_land), (4, u_near),
+        (5, outs.at[0, pl.ds(0, RING - 1)]), (6, outs.at[pl.ds(0, RING - 1)]), (7, grad_out),
+    ):
+        near(whole, whole, group, 1).wait_send()
+    row_cascade.finish(all_a.at[me])
+    send_cross(True)
+    u_cascade.finish(u_all.at[s])
     swap_ids.wait_send(ids_ref.at[pl.ds(0, GROUP - 1)])
     swap_cross.wait_send(cross_land)
     swap_mixed.wait_send(mixed_land)
@@ -522,6 +744,27 @@
         store.wait()
 
 
+def hand_over(
+    w_in, m_in, v_in, blocks_in, ids_in, w_out, m_out, v_out, blocks_out, ids_out, w_v, m_v, v_v, blocks_v, in_sem, out_sem
+):
+    arrays = ((m_in, m_v, m_out), (v_in, v_v, v_out), (blocks_in, blocks_v, blocks_out), (w_in, w_v, w_out))
+    fetches, stores = [], []
+    for array, (src, stage, dst) in enumerate(arrays):
+        half = src.shape[0] // 2
+        for k in range(2):
+            part = pl.ds(k * half, half)
+            fetches.append(pltpu.make_async_copy(src.at[part], stage.at[part], in_sem.at[2 * array + k]))
+            stores.append(pltpu.make_async_copy(stage.at[part], dst.at[part], out_sem.at[2 * array + k]))
+    for fetch in fetches:
+        fetch.start()
+    ids_out[...] = ids_in[:, 0, :].T[:CAP, :]
+    for fetch, store in zip(fetches, stores):
+        fetch.wait()
+        store.start()
+    for store in stores:
+        store.wait()
+
+
 def shards(section_inputs, top_grad, weights, first_moment, second_moment, block_list, block_owner):
     sections = lax.axis_size("section")
     model_width = section_inputs.shape[3]
@@ -529,21 +772,9 @@
     width = weights.shape[1]
     tokens = section_inputs.shape[1] * section_inputs.shape[2]
     chunk = sections * rank // GROUP
+    entries = block_list.shape[2]
     scale_a = model_width ** (-0.5)
     scale_b = rank ** (-0.5)
-
-    chosen = block_list[0, 0]
-    owners = block_owner[0, 0, :, 0]
-    positions = jnp.arange(chosen.shape[0], dtype=jnp.int32)
-    same_owner = (owners[None, :] == owners[:, None]) & (positions[None, :] < positions[:, None])
-    place = jnp.sum(same_owner.astype(jnp.int32), axis=1)
-    selector = (owners[None, :] * CAP + place[None, :]) == jnp.arange(GROUP * CAP, dtype=jnp.int32)[:, None]
-    slots = jnp.sum(jnp.where(selector, chosen[None, :] + 1, 0), axis=1) - 1
-    tile_count = width * 2 // BS
-    ids = jnp.where(slots >= 0, lax.axis_index("dp") * tile_count + slots, -1)
-    ids = jnp.broadcast_to(ids.reshape(GROUP, 1, CAP), (GROUP, 8, CAP))
-    ids = jnp.pad(ids, ((0, 0), (0, 0), (0, 128 - CAP)))
-    slots = jnp.pad(slots[None], ((0, 0), (0, 128 - GROUP * CAP)))
 
     any_spec = pl.BlockSpec(memory_space=pl.ANY)
     vmem = pl.BlockSpec(memory_space=pltpu.VMEM)
@@ -557,21 +788,28 @@
             jax.ShapeDtypeStruct((GROUP, CAP, BS, BS), BF16),
             jax.ShapeDtypeStruct((GROUP, 8, 128), jnp.int32),
         ),
-        in_specs=[any_spec] * 5 + [pl.BlockSpec(memory_space=pltpu.SMEM), vmem],
+        in_specs=[any_spec] * 5 + [pl.BlockSpec(memory_space=pltpu.SMEM)] * 2,
         out_specs=(any_spec,) * 5,
         scratch_shapes=[
-            pltpu.VMEM((tokens, model_width), BF16),
             pltpu.VMEM((tokens, model_width), BF16),
             pltpu.VMEM((2 * width, rank), BF16),
             pltpu.VMEM((2 * width, rank), F32),
             pltpu.VMEM((2 * width, rank), F32),
             pltpu.VMEM((2 * width, rank), F32),
             pltpu.VMEM((GROUP, width, rank), BF16),
-            pltpu.VMEM((GROUP, width, rank), BF16),
-            pltpu.VMEM((GROUP, rank, width), BF16),
             pltpu.VMEM((GROUP, rank, width), BF16),
             pltpu.VMEM((60, rank // 4, width), BF16),
-            pltpu.VMEM((60, rank // 4, width), BF16),
+            pltpu.VMEM((RING, width, rank), BF16),
+            pltpu.VMEM((RING, width, rank), BF16),
+            pltpu.VMEM((RING, tokens, width), BF16),
+            pltpu.VMEM((RING, RING, tokens, rank), BF16),
+            pltpu.VMEM((RING - 1, RING, tokens, rank), BF16),
+            pltpu.VMEM((RING - 1, tokens, rank), BF16),
+            pltpu.VMEM((RING - 1, tokens, rank), BF16),
+            pltpu.VMEM((RING, RING, rank, tokens), BF16),
+            pltpu.VMEM((RING - 1, rank, width), BF16),
+            pltpu.VMEM((RING, rank, width), BF16),
+            pltpu.VMEM((6, rank // 2, width), BF16),
             pltpu.VMEM((sections, width, rank), BF16),
             pltpu.VMEM((sections, sections * rank, rank), BF16),
             pltpu.VMEM((sections * rank, rank), BF16),
@@ -580,7 +818,6 @@
             pltpu.VMEM((GROUP - 1, chunk, rank), BF16),
             pltpu.VMEM((sections * rank, rank), BF16),
             pltpu.VMEM((tokens, rank), F32),
-            pltpu.VMEM((rank, tokens), BF16),
             pltpu.VMEM((tokens, rank), BF16),
             pltpu.VMEM((sections, rank, tokens), BF16),
             pltpu.VMEM((sections, rank, tokens), F32),
@@ -591,13 +828,15 @@
             pltpu.VMEM((GROUP, CAP, BS, BS), BF16),
             pltpu.VMEM((2 * width, rank), BF16),
             pltpu.VMEM((GROUP, 8, 128), jnp.int32),
+            pltpu.VMEM((GROUP, 8, 128), jnp.int32),
+            pltpu.SMEM((GROUP * CAP,), jnp.int32),
             dma((6,)),
-            dma((1,)), dma((40,)), dma((1,)), dma((40,)),
-            dma((1,)), dma((60,)), dma((1,)), dma((60,)),
+            dma((1,)), dma((40,)), dma((1,)), dma((4,)),
+            dma((1,)), dma((60,)), dma((1,)), dma((6,)),
+            dma((RING,)), dma((sections,)), dma((sections,)),
             dma((sections,)), dma((sections,)),
-            dma((sections,)), dma((sections,)),
-            dma((sections,)), dma((sections,)),
-            dma((6, 2)),
+            dma((RING,)), dma((sections,)), dma((sections,)),
+            dma((6, 2)), dma((8, RING)),
         ],
         compiler_params=pltpu.CompilerParams(
             collective_id=0, has_side_effects=True, vmem_limit_bytes=62 * 1024 * 1024
@@ -611,15 +850,27 @@
         weights.reshape(2 * width, rank),
         first_moment.reshape(2 * width, rank),
         second_moment.reshape(2 * width, rank),
-        slots,
-        ids,
+        block_list.reshape(1, entries),
+        block_owner.reshape(1, entries),
     )
+    results = (new_weights, new_first, new_second, blocks)
+    *results, got_ids = pl.pallas_call(
+        hand_over,
+        out_shape=(
+            *(jax.ShapeDtypeStruct(array.shape, array.dtype) for array in results),
+            jax.ShapeDtypeStruct((CAP, GROUP), jnp.int32),
+        ),
+        in_specs=[any_spec] * 4 + [vmem],
+        out_specs=(any_spec,) * 4 + (vmem,),
+        scratch_shapes=[pltpu.VMEM(array.shape, array.dtype) for array in results] + [dma((8,)), dma((8,))],
+    )(*results, got_ids)
+    new_weights, new_first, new_second, blocks = results
     return (
         new_weights.reshape(weights.shape),
         new_first.reshape(weights.shape),
         new_second.reshape(weights.shape),
         blocks[None, None],
-        got_ids[:, 0, :CAP][None, None],
+        got_ids.T[None, None],
     )
 
 

time: 150 us -> 133 us (0.89)
  local copies, waits for them, and re-layouts: 11.7 us -> 0 us
  Pallas kernels: 135 us -> 131 us
  other arithmetic: 2.33 us -> 0 us
    unnamed x4 -> x0, local copies, waits for them, and re-layouts: 9.02 us -> none
    pallas_call x1, Pallas kernels: 135 us -> 127 us  [shards(): pl.pallas_call(functools.partial(whole_kernel, sections, scale_a, scale_b...]
    pallas_call x0 -> x1, Pallas kernels: none -> 4.41 us  [shards(): pl.pallas_call(hand_over, out_shape=(*(jax.ShapeDtypeStruct(array.shape,...]
where the time goes in v3:
time: 133 us; the launch traced here: 132 us
  Pallas kernels  131 us (98%)
    pallas_call x1, Pallas kernels, shards(): pl.pallas_call(functools.partial(whole_kernel, sections, scale_a, scale_b...  127 us
    pallas_call x1, Pallas kernels, shards(): pl.pallas_call(hand_over, out_shape=(*(jax.ShapeDtypeStruct(array.shape,...  4.41 us

profile of v3, /device:TPU:0, one launch (start us, length us, event | category | flops | bytes accessed | tf_op | source)
XLA Modules:
  0.0 132.0 jit_solution(5090557644951920120)
XLA Ops:
  0.6 126.8 %shard_map.110 = (bf16[2048,128]{1,0:T(8,128)(2,1)}, f32[2048,128]{1,0:T(8,128)}, f32[2048,128]{1,0:T(8,128)}, bf16[16,2,128,128]{3,2,1,0:T(8,128)(2,1)}, s32[16,8,128]{2,1,0:T(8,128)}) custom-call(bf16[256,16384]{1,0:T(8,128)(2,1)} %bitcast.14, bf16[256,16384]{1,0:T(8,128)(2,1)} %bitcast.15, bf16[2048,128]{1,0:T(8,128)(2,1)} %bitcast.18, ...), custom_call_target="tpu_custom_call" | custom-call | flops 4294967296 | bytes 16777216 | tf_op jit(solution)/shard_map/pallas_call | solution.py:782
  127.4 4.4 %shard_map.111 = (bf16[2048,128]{1,0:T(8,128)(2,1)}, f32[2048,128]{1,0:T(8,128)}, f32[2048,128]{1,0:T(8,128)}, bf16[16,2,128,128]{3,2,1,0:T(8,128)(2,1)}, s32[2,16]{1,0:T(2,128)}) custom-call(bf16[2048,128]{1,0:T(8,128)(2,1)} %get-tuple-element.15.w_in, f32[2048,128]{1,0:T(8,128)} %get-tuple-element.16.m_in, f32[2048,128]{1,0:T(8,128)} %get-tuple-element.17.v_in, ...), custom_call_target="tpu_custom_call" | custom-call | tf_op jit(solution)/shard_map/pallas_call | solution.py:857

commit v4 on v3

--- a/solution.py
+++ b/solution.py
@@ -315,7 +315,7 @@
     rows_a, cross_all, cross_part, cross_land, mixed_part, mixed_land, mixed,
     acc, out_n, u_all, u_acc, deltas, total, relayed, tiles, outbox, w_new, ids_in, ids_ref, slot_ref,
     local_sem, ga_send, ga_recv, gb_send, gb_recv, sa_send, sa_recv, sb_send, sb_recv,
-    row_send, row_turn, row_recv, cross_send, cross_recv, u_send, u_turn_sem, u_recv, swap_sem, near_sem,
+    row_send, row_turn, row_recv, cross_send, cross_turn, cross_recv, u_send, u_turn_sem, u_recv, swap_sem, near_sem,
 ):
     s = lax.axis_index("section")
     plane = Plane()
@@ -367,24 +367,38 @@
             device_id={"section": to}, device_id_type=MESH,
         )
 
-    def send_cross(waiting):
+    def cross_copy(layer, sem, to):
+        block = cross_all.at[layer, pl.ds((layer + 1) * rank, (sections - 1 - layer) * rank)]
+        return down(block, block, sem, cross_recv.at[layer], to)
+
+    def cross_outgoing(act):
         for layer in range(1, sections - 1):
             @pl.when(s == layer)
             def _():
-                block = cross_all.at[layer, pl.ds((layer + 1) * rank, (sections - 1 - layer) * rank)]
-                for to in range(layer - 1, -1, -1):
-                    copy = down(block, block, cross_send.at[to], cross_recv.at[layer], to)
-                    if waiting:
-                        copy.wait_send()
-                    else:
-                        copy.start()
-
-    def wait_cross():
-        for layer in range(1, sections - 1):
-            @pl.when(layer > s)
+                for to in range(layer // 2 - 1, -1, -1):
+                    act(cross_copy(layer, cross_send.at[to], 2 * to + layer % 2))
+                if layer % 2 == 1:
+                    act(cross_copy(layer, cross_send.at[RING - 1], layer - 1))
+
+    def cross_relay():
+        for layer in range(sections - 2, 1, -1):
+            @pl.when((layer // 2 > level) & (core == layer % 2))
             def _():
-                block = cross_all.at[layer, pl.ds((layer + 1) * rank, (sections - 1 - layer) * rank)]
-                down(block, block, cross_send.at[layer], cross_recv.at[layer], layer).wait_recv()
+                cross_copy(layer, cross_turn.at[layer], s + 1 - 2 * core).wait_recv()
+                cross_copy(layer, cross_turn.at[layer], s + 1 - 2 * core).start()
+
+    def cross_rest():
+        for layer in range(sections - 2, 0, -1):
+            @pl.when((layer > s) & ((layer // 2 == level) | (core != layer % 2)))
+            def _():
+                cross_copy(layer, cross_turn.at[layer], s + 1 - 2 * core).wait_recv()
+
+    def cross_finish():
+        cross_outgoing(lambda copy: copy.wait_send())
+        for layer in range(sections - 2, 1, -1):
+            @pl.when((layer // 2 > level) & (core == layer % 2))
+            def _():
+                cross_copy(layer, cross_turn.at[layer], s + 1 - 2 * core).wait_send()
 
     class Cascade:
         def __init__(self, blocks, send_sem, turn_sem, recv_sem):
@@ -566,6 +580,9 @@
 
     lax.fori_loop(0, GROUP // 2, forward_a, 0)
 
+    spread_cross.wait_recv(cross_all.at[s, pl.ds(0, (GROUP - 1) * chunk)])
+    cross_outgoing(lambda copy: copy.start())
+
     for n, k in enumerate(HOPS):
         across(u_part.at[n], u_land.at[n], 3, RING - k).wait_recv()
 
@@ -588,8 +605,6 @@
     for k in HOPS:
         near(outs.at[level, x], outs.at[level, x], 5, k).start()
 
-    spread_cross.wait_recv(cross_all.at[s, pl.ds(0, (GROUP - 1) * chunk)])
-    send_cross(False)
 
     def backward(left, right, part, q):
         cols = pl.ds(pl.multiple_of(q * width, width), width)
@@ -609,7 +624,8 @@
         near(spot, spot, 5, k).wait_recv()
     for k in HOPS:
         across(outs.at[level], outs.at[level], 6, k).start()
-    wait_cross()
+    cross_relay()
+    cross_rest()
     u_cascade.relay()
     u_cascade.rest()
     for layer in range(sections):
@@ -628,10 +644,6 @@
                         cross_all[lower, layer * rank:(layer + 1) * rank], delta, preferred_element_type=F32
                     )
 
-    for dz, dx in order:
-        backward(deltas[s], h_v, part_a, plane.away(dz, dx))
-        scatter_a.send_chunk(dz, dx)
-
     for layer in range(sections):
         @pl.when(layer > s)
         def _():
@@ -644,6 +656,10 @@
             mixed_part[layer * rank:(layer + 1) * rank] = jnp.zeros((rank, rank), BF16)
     swap_mixed.start(lambda q: piece(mixed_part, q), lambda k: mixed_land.at[k - 1])
 
+    for dz, dx in order[:7]:
+        backward(deltas[s], h_v, part_a, plane.away(dz, dx))
+        scatter_a.send_chunk(dz, dx)
+
     def top_grad_of(layer_level):
         summed = jnp.dot(outs[layer_level, 0], merged[0], preferred_element_type=F32)
         for spot in range(1, RING):
@@ -656,6 +672,10 @@
         grad_out[n] = top_grad_of(wrap(level - k))
         across(grad_out.at[n], part_b.at[level], 7, RING - k).start()
     part_b[level] = top_grad_of(level)
+    for dz, dx in order[7:]:
+        backward(deltas[s], h_v, part_a, plane.away(dz, dx))
+        scatter_a.send_chunk(dz, dx)
+
     swap_mixed.wait_recv(mixed_land)
     mixed_sum = mixed_part[own_rows].astype(F32)
     for k in range(GROUP - 1):
@@ -701,11 +721,14 @@
     scatter_a.result(total)
     adam(0, lambda rows: total[:, rows].T * scale_a)
 
-    for k in range(GROUP * CAP):
-        index = slot_ref[k]
-        tile = tiles[jnp.maximum(index, 0)]
-        outbox[k // CAP, k % CAP] = jnp.where(index >= 0, tile, jnp.zeros_like(tile))
-    swap_tiles.start(lambda q: outbox.at[q], lambda k: blocks_out.at[me])
+    for k in range(1, GROUP + 1):
+        owner = lax.rem(me + k, GROUP)
+        for place in range(CAP):
+            index = slot_ref[owner * CAP + place]
+            tile = tiles[jnp.maximum(index, 0)]
+            outbox[owner, place] = jnp.where(index >= 0, tile, jnp.zeros_like(tile))
+        if k < GROUP:
+            swap_tiles.copy(outbox.at[owner], blocks_out.at[me], owner).start()
     kept = pltpu.make_async_copy(outbox.at[me], blocks_out.at[me], local_sem.at[5])
     kept.start()
     w_new[...] = wide[...].astype(BF16)
@@ -730,7 +753,7 @@
     ):
         near(whole, whole, group, 1).wait_send()
     row_cascade.finish(all_a.at[me])
-    send_cross(True)
+    cross_finish()
     u_cascade.finish(u_all.at[s])
     swap_ids.wait_send(ids_ref.at[pl.ds(0, GROUP - 1)])
     swap_cross.wait_send(cross_land)
@@ -834,7 +857,7 @@
             dma((1,)), dma((40,)), dma((1,)), dma((4,)),
             dma((1,)), dma((60,)), dma((1,)), dma((6,)),
             dma((RING,)), dma((sections,)), dma((sections,)),
-            dma((sections,)), dma((sections,)),
+            dma((RING,)), dma((sections,)), dma((sections,)),
             dma((RING,)), dma((sections,)), dma((sections,)),
             dma((6, 2)), dma((8, RING)),
         ],

time: 133 us -> 130 us (0.977)
  Pallas kernels: 131 us -> 129 us
    pallas_call x1, Pallas kernels: 127 us -> 124 us  [shards(): pl.pallas_call(functools.partial(whole_kernel, sections, scale_a, scale_b...]
where the time goes in v4:
time: 130 us
  Pallas kernels  129 us (99%)
    pallas_call x1, Pallas kernels, shards(): pl.pallas_call(functools.partial(whole_kernel, sections, scale_a, scale_b...  124 us
    pallas_call x1, Pallas kernels, shards(): pl.pallas_call(hand_over, out_shape=(*(jax.ShapeDtypeStruct(array.shape,...  4.41 us

profile of v4, /device:TPU:0, one launch (start us, length us, event | category | flops | bytes accessed | tf_op | source)
XLA Modules:
  0.0 129.6 jit_solution(9901451715073511346)
XLA Ops:
  0.6 124.4 %shard_map.110 = (bf16[2048,128]{1,0:T(8,128)(2,1)}, f32[2048,128]{1,0:T(8,128)}, f32[2048,128]{1,0:T(8,128)}, bf16[16,2,128,128]{3,2,1,0:T(8,128)(2,1)}, s32[16,8,128]{2,1,0:T(8,128)}) custom-call(bf16[256,16384]{1,0:T(8,128)(2,1)} %bitcast.14, bf16[256,16384]{1,0:T(8,128)(2,1)} %bitcast.15, bf16[2048,128]{1,0:T(8,128)(2,1)} %bitcast.18, ...), custom_call_target="tpu_custom_call" | custom-call | flops 4294967296 | bytes 16777216 | tf_op jit(solution)/shard_map/pallas_call | solution.py:805
  125.0 4.4 %shard_map.111 = (bf16[2048,128]{1,0:T(8,128)(2,1)}, f32[2048,128]{1,0:T(8,128)}, f32[2048,128]{1,0:T(8,128)}, bf16[16,2,128,128]{3,2,1,0:T(8,128)(2,1)}, s32[2,16]{1,0:T(2,128)}) custom-call(bf16[2048,128]{1,0:T(8,128)(2,1)} %get-tuple-element.15.w_in, f32[2048,128]{1,0:T(8,128)} %get-tuple-element.16.m_in, f32[2048,128]{1,0:T(8,128)} %get-tuple-element.17.v_in, ...), custom_call_target="tpu_custom_call" | custom-call | tf_op jit(solution)/shard_map/pallas_call | solution.py:880

commit v5 on v4

--- a/solution.py
+++ b/solution.py
@@ -654,7 +654,31 @@
         @pl.when(layer <= s)
         def _():
             mixed_part[layer * rank:(layer + 1) * rank] = jnp.zeros((rank, rank), BF16)
-    swap_mixed.start(lambda q: piece(mixed_part, q), lambda k: mixed_land.at[k - 1])
+    owns_rows = me * chunk // rank > s
+    for k in range(1, GROUP):
+        to = lax.rem(me + k, GROUP)
+
+        @pl.when(to * chunk // rank > s)
+        def _():
+            swap_mixed.copy(piece(mixed_part, to), mixed_land.at[k - 1], to).start()
+
+    for layer in range(sections):
+        @pl.when(layer <= s)
+        def _():
+            mixed[layer * rank:(layer + 1) * rank] = jnp.zeros((rank, rank), BF16)
+
+    def mixed_waits(wait):
+        for layer in range(sections - 1):
+            filled = (sections - 1 - layer) * rank
+
+            @pl.when((s == layer) & owns_rows)
+            def _():
+                wait(mixed.at[pl.ds(0, filled - chunk)])
+
+            @pl.when((s == layer) & jnp.logical_not(owns_rows))
+            def _():
+                wait(mixed.at[pl.ds(0, filled)])
+
 
     for dz, dx in order[:7]:
         backward(deltas[s], h_v, part_a, plane.away(dz, dx))
@@ -676,12 +700,15 @@
         backward(deltas[s], h_v, part_a, plane.away(dz, dx))
         scatter_a.send_chunk(dz, dx)
 
-    swap_mixed.wait_recv(mixed_land)
-    mixed_sum = mixed_part[own_rows].astype(F32)
-    for k in range(GROUP - 1):
-        mixed_sum = mixed_sum + mixed_land[k].astype(F32)
-    mixed[own_rows] = mixed_sum.astype(BF16)
-    spread_mixed.start(lambda q: mixed.at[own_rows], lambda k: mixed.at[own_rows])
+    @pl.when(owns_rows)
+    def _():
+        swap_mixed.wait_recv(mixed_land)
+        mixed_sum = mixed_part[own_rows].astype(F32)
+        for k in range(GROUP - 1):
+            mixed_sum = mixed_sum + mixed_land[k].astype(F32)
+        mixed[own_rows] = mixed_sum.astype(BF16)
+        spread_mixed.start(lambda q: mixed.at[own_rows], lambda k: mixed.at[own_rows])
+
     for a in (2, 1, 3, 0):
         scatter_a.pass_on(a)
     for k in HOPS:
@@ -692,7 +719,7 @@
         scatter_a.settle(a)
     ring_sum.sum_pass()
     scatter_a.pass_last()
-    spread_mixed.wait_recv(mixed.at[pl.ds(0, (GROUP - 1) * chunk)])
+    mixed_waits(spread_mixed.wait_recv)
     loads[2].wait()
     loads[3].wait()
 
@@ -757,9 +784,13 @@
     u_cascade.finish(u_all.at[s])
     swap_ids.wait_send(ids_ref.at[pl.ds(0, GROUP - 1)])
     swap_cross.wait_send(cross_land)
-    swap_mixed.wait_send(mixed_land)
+    mixed_waits(swap_mixed.wait_send)
     spread_cross.wait_send(mixed.at[pl.ds(0, (GROUP - 1) * chunk)])
-    spread_mixed.wait_send(mixed.at[pl.ds(0, (GROUP - 1) * chunk)])
+
+    @pl.when(owns_rows)
+    def _():
+        spread_mixed.wait_send(mixed.at[pl.ds(0, (GROUP - 1) * chunk)])
+
     swap_tiles.wait_send(outbox.at[pl.ds(0, GROUP - 1)])
     swap_tiles.wait_recv(blocks_out.at[pl.ds(0, GROUP - 1)])
     kept.wait()

time: 130 us -> 129 us (level)
  no operation moved by 1% of the time
where the time goes in v5:
time: 129 us
  Pallas kernels  128 us (99%)
    pallas_call x1, Pallas kernels, shards(): pl.pallas_call(functools.partial(whole_kernel, sections, scale_a, scale_b...  124 us
    pallas_call x1, Pallas kernels, shards(): pl.pallas_call(hand_over, out_shape=(*(jax.ShapeDtypeStruct(array.shape,...  4.41 us

profile of v5, /device:TPU:0, one launch (start us, length us, event | category | flops | bytes accessed | tf_op | source)
XLA Modules:
  0.0 128.7 jit_solution(12013598009220899885)
XLA Ops:
  0.6 123.5 %shard_map.110 = (bf16[2048,128]{1,0:T(8,128)(2,1)}, f32[2048,128]{1,0:T(8,128)}, f32[2048,128]{1,0:T(8,128)}, bf16[16,2,128,128]{3,2,1,0:T(8,128)(2,1)}, s32[16,8,128]{2,1,0:T(8,128)}) custom-call(bf16[256,16384]{1,0:T(8,128)(2,1)} %bitcast.14, bf16[256,16384]{1,0:T(8,128)(2,1)} %bitcast.15, bf16[2048,128]{1,0:T(8,128)(2,1)} %bitcast.18, ...), custom_call_target="tpu_custom_call" | custom-call | flops 4294967296 | bytes 16777216 | tf_op jit(solution)/shard_map/pallas_call | solution.py:836
  124.2 4.4 %shard_map.111 = (bf16[2048,128]{1,0:T(8,128)(2,1)}, f32[2048,128]{1,0:T(8,128)}, f32[2048,128]{1,0:T(8,128)}, bf16[16,2,128,128]{3,2,1,0:T(8,128)(2,1)}, s32[2,16]{1,0:T(2,128)}) custom-call(bf16[2048,128]{1,0:T(8,128)(2,1)} %get-tuple-element.15.w_in, f32[2048,128]{1,0:T(8,128)} %get-tuple-element.16.m_in, f32[2048,128]{1,0:T(8,128)} %get-tuple-element.17.v_in, ...), custom_call_target="tpu_custom_call" | custom-call | tf_op jit(solution)/shard_map/pallas_call | solution.py:911
